TPU v7x, 128 devices: a whole 4x4x4 slice. The times are simulated.
128 devices in a mesh: head: 8 (over x_lo, z), inner: 4 (over y), outer: 4 (over x_hi, core).
Axes of the slice: x: 4 (x_hi: 2, x_lo: 2; x = x_hi * 2 + x_lo), y: 4, z: 4, core: 2. Of those that a mesh axis runs over, the one named last changes fastest.
Arguments:
- queries: bfloat16 [16, 1024, 2048], P(('inner', 'outer'), 'head'), may hold values from -6 to 6
- key_input: bfloat16 [16, 1024, 1024], P(('inner', 'outer'), 'head'), may hold values from -6 to 6
- value_input: bfloat16 [16, 1024, 1024], P(('inner', 'outer'), 'head'), may hold values from -6 to 6
- outputs: bfloat16 [16, 1024, 2048], P(('inner', 'outer'), 'head'), may hold values from -6 to 6
- output_gradient: bfloat16 [16, 1024, 2048], P(('inner', 'outer'), 'head'), may hold values from -6 to 6
- log_sum_exp: float32 [16, 1024, 16], P(('inner', 'outer'), 'head'), may hold values from -1 to 16
- block_order: int32 [32], replicated, may hold values from 0 to 31, as said below
Outputs:
- query_grad: bfloat16 [16, 1024, 2048], P(('inner', 'outer'), 'head')
- key_gradient: bfloat16 [16, 1024, 1024], P(('inner', 'outer'), 'head')
- value_gradient: bfloat16 [16, 1024, 1024], P(('inner', 'outer'), 'head')
Inputs may be any that keep to these rules, and one draw needn't show every extreme that they name: `block_order`: A permutation of the 32 sequence blocks in which storage blocks 2 c and 2 c + 1 hold blocks b and 31 - b for some b below 16.
All inputs are finite; a program needn't handle non-finite values.
Results may differ from a plain program's by a relative error of at most 0.0052.
Values may be sent and summed in bfloat16 or wider, within the bound.
A program may use at most 64 MiB of HBM per device.

v0:
```python
import jax
import jax.numpy as jnp
from jax import lax
from jax.sharding import PartitionSpec as P

QUERY_HEADS = 16
KEY_VALUE_HEADS = 8
HEAD_SIZE = 128


def from_behind(block, axis, distance):
    devices = range(lax.axis_size(axis))
    route = [((i - distance) % len(devices), i) for i in devices]
    return lax.ppermute(block, axis, route)


def block_rows(block_order, context_index, length):
    pair_ids = lax.dynamic_slice_in_dim(block_order, 2 * context_index, 2)
    middle = length // 2
    row_ids = jnp.arange(length, dtype=jnp.int32)
    placed = jnp.where(
        row_ids < middle, pair_ids[0] * middle + row_ids, pair_ids[1] * middle + row_ids - middle
    )
    return (placed, pair_ids)


def attend(
    query_rows,
    grad_rows,
    norm_rows,
    delta_rows,
    query_places,
    key_row_block,
    value_row_block,
    key_places,
):
    length = query_rows.shape[0]
    kv_heads = key_row_block.shape[1]
    heads_per_group = query_rows.shape[1] // kv_heads
    query_groups = query_rows.reshape(length, kv_heads, heads_per_group, HEAD_SIZE)
    grad_groups = grad_rows.reshape(length, kv_heads, heads_per_group, HEAD_SIZE)
    norm_groups = jnp.transpose(norm_rows.reshape(length, kv_heads, heads_per_group), (1, 2, 0))
    delta_groups = jnp.transpose(delta_rows.reshape(length, kv_heads, heads_per_group), (1, 2, 0))
    scores = jnp.einsum(
        "qhgd,khd->hgqk", query_groups, key_row_block, preferred_element_type=jnp.float32
    ) * HEAD_SIZE ** (-0.5)
    visible = key_places[None, :] <= query_places[:, None]
    probs = jnp.where(visible, jnp.exp(scores - norm_groups[..., None]), 0.0)
    prob_grad = jnp.einsum(
        "qhgd,khd->hgqk", grad_groups, value_row_block, preferred_element_type=jnp.float32
    )
    score_grad = (probs * (prob_grad - delta_groups[..., None])).astype(jnp.bfloat16)
    probs_low = probs.astype(jnp.bfloat16)
    query_part = jnp.einsum(
        "hgqk,khd->qhgd", score_grad, key_row_block, preferred_element_type=jnp.float32
    )
    key_part = jnp.einsum(
        "hgqk,qhgd->khd", score_grad, query_groups, preferred_element_type=jnp.float32
    )
    value_part = jnp.einsum(
        "hgqk,qhgd->khd", probs_low, grad_groups, preferred_element_type=jnp.float32
    )
    return (query_part.reshape(length, kv_heads * heads_per_group, HEAD_SIZE), key_part, value_part)


def contribute(
    statistics, key_row_block, value_row_block, query_pair, key_pair, query_places, key_places
):
    query_rows, grad_rows, norm_rows, delta_rows = statistics
    middle = query_rows.shape[0] // 2
    query_zero = jnp.zeros((middle,) + query_rows.shape[1:], jnp.float32)
    key_zero = jnp.zeros((middle,) + key_row_block.shape[1:], jnp.float32)
    query_halves = [query_zero, query_zero]
    key_halves = [key_zero, key_zero]
    value_halves = [key_zero, key_zero]
    for query_side in range(2):
        lower = query_side * middle
        for key_side in range(2):
            start = key_side * middle

            def run_pair(operand, lower=lower, start=start):
                return attend(
                    query_rows[lower : lower + middle],
                    grad_rows[lower : lower + middle],
                    norm_rows[lower : lower + middle],
                    delta_rows[lower : lower + middle],
                    query_places[lower : lower + middle],
                    key_row_block[start : start + middle],
                    value_row_block[start : start + middle],
                    key_places[start : start + middle],
                )

            def skip_pair(operand):
                return (query_zero, key_zero, key_zero)

            found = lax.cond(key_pair[key_side] <= query_pair[query_side], run_pair, skip_pair, 0)
            query_halves[query_side] = query_halves[query_side] + found[0]
            key_halves[key_side] = key_halves[key_side] + found[1]
            value_halves[key_side] = value_halves[key_side] + found[2]
    return (
        jnp.concatenate(query_halves, axis=0),
        jnp.concatenate(key_halves, axis=0),
        jnp.concatenate(value_halves, axis=0),
    )


def per_device(queries, key_input, value_input, outputs, output_gradient, log_sum_exp, block_order):
    local_row_count = queries.shape[1]
    query_rows = queries.reshape(local_row_count, QUERY_HEADS, HEAD_SIZE)
    key_row_block = key_input.reshape(local_row_count, KEY_VALUE_HEADS, HEAD_SIZE)
    value_row_block = value_input.reshape(local_row_count, KEY_VALUE_HEADS, HEAD_SIZE)
    grad_rows = output_gradient.reshape(local_row_count, QUERY_HEADS, HEAD_SIZE)
    row_delta = jnp.sum(
        grad_rows.astype(jnp.float32)
        * outputs.reshape(local_row_count, QUERY_HEADS, HEAD_SIZE).astype(jnp.float32),
        axis=2,
    )
    query_heads, key_heads, value_heads, grad_heads = (
        lax.all_to_all(query_rows, "head", split_axis=1, concat_axis=0, tiled=True),
        lax.all_to_all(key_row_block, "head", split_axis=1, concat_axis=0, tiled=True),
        lax.all_to_all(value_row_block, "head", split_axis=1, concat_axis=0, tiled=True),
        lax.all_to_all(grad_rows, "head", split_axis=1, concat_axis=0, tiled=True),
    )
    norm_heads, delta_heads = (
        lax.all_to_all(
            log_sum_exp.reshape(local_row_count, QUERY_HEADS),
            "head",
            split_axis=1,
            concat_axis=0,
            tiled=True,
        ),
        lax.all_to_all(row_delta, "head", split_axis=1, concat_axis=0, tiled=True),
    )
    length = query_heads.shape[0]
    context_index = lax.axis_index(("inner", "outer"))
    query_places, query_pair = block_rows(block_order, context_index, length)
    statistics = (query_heads, grad_heads, norm_heads, delta_heads)

    def absorb(anchor, carried):
        query_acc, keys_held, values_held, key_gradient_total, value_gradient_total = carried
        key_places, key_pair = block_rows(block_order, anchor, length)
        query_part, key_part, value_part = contribute(
            statistics, keys_held, values_held, query_pair, key_pair, query_places, key_places
        )
        return (
            query_acc + query_part,
            keys_held,
            values_held,
            key_gradient_total + key_part,
            value_gradient_total + value_part,
        )

    initial = (
        jnp.zeros(query_heads.shape, jnp.float32),
        key_heads,
        value_heads,
        jnp.zeros(key_heads.shape, jnp.float32),
        jnp.zeros(key_heads.shape, jnp.float32),
    )
    group_count = lax.axis_size(("inner", "outer"))

    def joined_turn(joined_step, state_now):
        anchor = (context_index - joined_step) % group_count
        query_acc, keys_held, values_held, key_gradient_total, value_gradient_total = absorb(
            anchor, state_now
        )
        keys_held, values_held = from_behind((keys_held, values_held), ("inner", "outer"), 1)
        key_gradient_total, value_gradient_total = from_behind(
            (key_gradient_total, value_gradient_total), ("inner", "outer"), 1
        )
        return (query_acc, keys_held, values_held, key_gradient_total, value_gradient_total)

    finished = lax.fori_loop(0, group_count, joined_turn, initial)
    query_acc, keys_held, values_held, key_gradient_total, value_gradient_total = finished
    score_scale = HEAD_SIZE ** (-0.5)
    gradients = (
        (query_acc * score_scale).astype(jnp.bfloat16),
        (key_gradient_total * score_scale).astype(jnp.bfloat16),
        value_gradient_total.astype(jnp.bfloat16),
    )
    query_back, key_gradient_local, value_gradient_local = (
        lax.all_to_all(gradients[0], "head", split_axis=0, concat_axis=1, tiled=True),
        lax.all_to_all(gradients[1], "head", split_axis=0, concat_axis=1, tiled=True),
        lax.all_to_all(gradients[2], "head", split_axis=0, concat_axis=1, tiled=True),
    )
    return (
        query_back.reshape(1, local_row_count, QUERY_HEADS * HEAD_SIZE),
        key_gradient_local.reshape(1, local_row_count, KEY_VALUE_HEADS * HEAD_SIZE),
        value_gradient_local.reshape(1, local_row_count, KEY_VALUE_HEADS * HEAD_SIZE),
    )


def solution(mesh):
    in_specs = (
        P(("inner", "outer"), "head", None),
        P(("inner", "outer"), "head", None),
        P(("inner", "outer"), "head", None),
        P(("inner", "outer"), "head", None),
        P(("inner", "outer"), "head", None),
        P(("inner", "outer"), "head", None),
        P(),
    )
    out_specs = (
        P(("inner", "outer"), "head", None),
        P(("inner", "outer"), "head", None),
        P(("inner", "outer"), "head", None),
    )
    return jax.shard_map(
        per_device, mesh=mesh, in_specs=in_specs, out_specs=out_specs, check_vma=False
    )
```

profile of v0, /device:TPU:0, one launch (start us, length us, event | category | flops | bytes accessed | tf_op | source)
XLA Modules:
  0.0 854.3 jit_solution(16413574826604632512)
XLA Ops:
  0.6 6.5 all-to-all-start.3
  13.3 4.7 all-to-all-start.5
  18.9 5.4 all-to-all-done.5
  24.2 4.1 all-to-all-start
  28.6 6.9 all-to-all-done
  35.5 11.2 %all_to_all.155 = bf16[128,16,128]{0,2,1:T(8,128)(2,1)S(1)} all-to-all(bf16[128,16,128]{0,2,1:T(8,128)(2,1)S(1)} %bitcast.356), channel_id=1, replica_groups=mesh['head'=8,'inner'=4,'outer'=4] {'head'}, dimensions={1} | all-to-all | bytes 1048576 | tf_op jit(solution)/shard_map/all_to_all | solution.py:119
  46.7 3.5 all-to-all-start.4
  51.0 7.4 all-to-all-done.4
  58.4 4.1 all-to-all-start.1
  65.0 4.7 all-to-all-done.1
  71.4 744.1 %while.24 = (s32[]{:T(128)}, f32[1024,2,128]{2,0,1:T(8,128)}, bf16[1024,1,128]{2,0,1:T(8,128)(2,1)}, bf16[1024,1,128]{2,0,1:T(8,128)(2,1)}, f32[1024,1,128]{2,0,...) while((s32[]{:T(128)}, f32[1024,2,128]{2,0,1:T(8,128)}, ...), condition=%wide.region_10.11_spmd.clone, body=%wide.region_1.10_spmd.clone.sunk | while | flops 2701928448 | bytes 77227000 | solution.py:173
  82.0 3.4 conditional.14
  98.5 2.8 collective-permute-start.3
  105.6 11.9 %collective-permute-done = bf16[1024,1,128]{2,0,1:T(8,128)(2,1)} collective-permute-done((bf16[1024,1,128]{2,0,1:T(8,128)(2,1)S(1)}, bf16[1024,1,128]{2,0,1:T(8,128)(2,1)}, u32[]{:S(2)}, u32[]{:S(2)}) %collective-permute-start) | collective-permute-done | bytes 262176 | tf_op jit(solution)/shard_map/while/body/eval_jaxpr/ppermute | solution.py:14
  117.5 2.8 collective-permute-done.1
  131.0 3.4 conditional.14
  145.6 2.8 collective-permute-start.1
  151.9 11.9 %collective-permute-done = bf16[1024,1,128]{2,0,1:T(8,128)(2,1)} collective-permute-done((bf16[1024,1,128]{2,0,1:T(8,128)(2,1)S(1)}, bf16[1024,1,128]{2,0,1:T(8,128)(2,1)}, u32[]{:S(2)}, u32[]{:S(2)}) %collective-permute-start) | collective-permute-done | bytes 262176 | tf_op jit(solution)/shard_map/while/body/eval_jaxpr/ppermute | solution.py:14
  177.3 3.4 conditional.14
  197.1 13.1 %collective-permute-done = bf16[1024,1,128]{2,0,1:T(8,128)(2,1)} collective-permute-done((bf16[1024,1,128]{2,0,1:T(8,128)(2,1)S(1)}, bf16[1024,1,128]{2,0,1:T(8,128)(2,1)}, u32[]{:S(2)}, u32[]{:S(2)}) %collective-permute-start) | collective-permute-done | bytes 262176 | tf_op jit(solution)/shard_map/while/body/eval_jaxpr/ppermute | solution.py:14
  210.2 2.8 collective-permute-done.1
  242.2 14.3 %collective-permute-done = bf16[1024,1,128]{2,0,1:T(8,128)(2,1)} collective-permute-done((bf16[1024,1,128]{2,0,1:T(8,128)(2,1)S(1)}, bf16[1024,1,128]{2,0,1:T(8,128)(2,1)}, u32[]{:S(2)}, u32[]{:S(2)}) %collective-permute-start) | collective-permute-done | bytes 262176 | tf_op jit(solution)/shard_map/while/body/eval_jaxpr/ppermute | solution.py:14
  256.6 2.8 collective-permute-done.1
  287.5 15.4 %collective-permute-done = bf16[1024,1,128]{2,0,1:T(8,128)(2,1)} collective-permute-done((bf16[1024,1,128]{2,0,1:T(8,128)(2,1)S(1)}, bf16[1024,1,128]{2,0,1:T(8,128)(2,1)}, u32[]{:S(2)}, u32[]{:S(2)}) %collective-permute-start) | collective-permute-done | bytes 262176 | tf_op jit(solution)/shard_map/while/body/eval_jaxpr/ppermute | solution.py:14
  316.3 3.4 conditional.14
  333.9 15.4 %collective-permute-done = bf16[1024,1,128]{2,0,1:T(8,128)(2,1)} collective-permute-done((bf16[1024,1,128]{2,0,1:T(8,128)(2,1)S(1)}, bf16[1024,1,128]{2,0,1:T(8,128)(2,1)}, u32[]{:S(2)}, u32[]{:S(2)}) %collective-permute-start) | collective-permute-done | bytes 262176 | tf_op jit(solution)/shard_map/while/body/eval_jaxpr/ppermute | solution.py:14
  349.2 2.8 collective-permute-done.1
  362.7 3.4 conditional.14
  380.2 15.4 %collective-permute-done = bf16[1024,1,128]{2,0,1:T(8,128)(2,1)} collective-permute-done((bf16[1024,1,128]{2,0,1:T(8,128)(2,1)S(1)}, bf16[1024,1,128]{2,0,1:T(8,128)(2,1)}, u32[]{:S(2)}, u32[]{:S(2)}) %collective-permute-start) | collective-permute-done | bytes 262176 | tf_op jit(solution)/shard_map/while/body/eval_jaxpr/ppermute | solution.py:14
  426.5 15.4 %collective-permute-done = bf16[1024,1,128]{2,0,1:T(8,128)(2,1)} collective-permute-done((bf16[1024,1,128]{2,0,1:T(8,128)(2,1)S(1)}, bf16[1024,1,128]{2,0,1:T(8,128)(2,1)}, u32[]{:S(2)}, u32[]{:S(2)}) %collective-permute-start) | collective-permute-done | bytes 262176 | tf_op jit(solution)/shard_map/while/body/eval_jaxpr/ppermute | solution.py:14
  472.9 15.4 %collective-permute-done = bf16[1024,1,128]{2,0,1:T(8,128)(2,1)} collective-permute-done((bf16[1024,1,128]{2,0,1:T(8,128)(2,1)S(1)}, bf16[1024,1,128]{2,0,1:T(8,128)(2,1)}, u32[]{:S(2)}, u32[]{:S(2)}) %collective-permute-start) | collective-permute-done | bytes 262176 | tf_op jit(solution)/shard_map/while/body/eval_jaxpr/ppermute | solution.py:14
  501.7 3.4 conditional.14
  519.2 15.4 %collective-permute-done = bf16[1024,1,128]{2,0,1:T(8,128)(2,1)} collective-permute-done((bf16[1024,1,128]{2,0,1:T(8,128)(2,1)S(1)}, bf16[1024,1,128]{2,0,1:T(8,128)(2,1)}, u32[]{:S(2)}, u32[]{:S(2)}) %collective-permute-start) | collective-permute-done | bytes 262176 | tf_op jit(solution)/shard_map/while/body/eval_jaxpr/ppermute | solution.py:14
  565.6 15.4 %collective-permute-done = bf16[1024,1,128]{2,0,1:T(8,128)(2,1)} collective-permute-done((bf16[1024,1,128]{2,0,1:T(8,128)(2,1)S(1)}, bf16[1024,1,128]{2,0,1:T(8,128)(2,1)}, u32[]{:S(2)}, u32[]{:S(2)}) %collective-permute-start) | collective-permute-done | bytes 262176 | tf_op jit(solution)/shard_map/while/body/eval_jaxpr/ppermute | solution.py:14
  611.9 15.4 %collective-permute-done = bf16[1024,1,128]{2,0,1:T(8,128)(2,1)} collective-permute-done((bf16[1024,1,128]{2,0,1:T(8,128)(2,1)S(1)}, bf16[1024,1,128]{2,0,1:T(8,128)(2,1)}, u32[]{:S(2)}, u32[]{:S(2)}) %collective-permute-start) | collective-permute-done | bytes 262176 | tf_op jit(solution)/shard_map/while/body/eval_jaxpr/ppermute | solution.py:14
  658.2 15.4 %collective-permute-done = bf16[1024,1,128]{2,0,1:T(8,128)(2,1)} collective-permute-done((bf16[1024,1,128]{2,0,1:T(8,128)(2,1)S(1)}, bf16[1024,1,128]{2,0,1:T(8,128)(2,1)}, u32[]{:S(2)}, u32[]{:S(2)}) %collective-permute-start) | collective-permute-done | bytes 262176 | tf_op jit(solution)/shard_map/while/body/eval_jaxpr/ppermute | solution.py:14
  687.1 3.4 conditional.14
  704.6 15.4 %collective-permute-done = bf16[1024,1,128]{2,0,1:T(8,128)(2,1)} collective-permute-done((bf16[1024,1,128]{2,0,1:T(8,128)(2,1)S(1)}, bf16[1024,1,128]{2,0,1:T(8,128)(2,1)}, u32[]{:S(2)}, u32[]{:S(2)}) %collective-permute-start) | collective-permute-done | bytes 262176 | tf_op jit(solution)/shard_map/while/body/eval_jaxpr/ppermute | solution.py:14
  733.4 3.4 conditional.14
  750.9 15.4 %collective-permute-done = bf16[1024,1,128]{2,0,1:T(8,128)(2,1)} collective-permute-done((bf16[1024,1,128]{2,0,1:T(8,128)(2,1)S(1)}, bf16[1024,1,128]{2,0,1:T(8,128)(2,1)}, u32[]{:S(2)}, u32[]{:S(2)}) %collective-permute-start) | collective-permute-done | bytes 262176 | tf_op jit(solution)/shard_map/while/body/eval_jaxpr/ppermute | solution.py:14
  779.7 3.4 conditional.14
  797.3 15.4 %collective-permute-done = bf16[1024,1,128]{2,0,1:T(8,128)(2,1)} collective-permute-done((bf16[1024,1,128]{2,0,1:T(8,128)(2,1)S(1)}, bf16[1024,1,128]{2,0,1:T(8,128)(2,1)}, u32[]{:S(2)}, u32[]{:S(2)}) %collective-permute-start) | collective-permute-done | bytes 262176 | tf_op jit(solution)/shard_map/while/body/eval_jaxpr/ppermute | solution.py:14
  818.6 3.6 all-to-all-start.8
  824.9 5.5 all-to-all-done.8
  830.5 3.4 all-to-all-start.7
  836.6 4.5 all-to-all-done.7
  841.1 3.5 all-to-all-start.6
  847.3 5.5 all-to-all-done.6
  (1042 shorter events, 479.3 us)
Async XLA Ops:
  96.6 23.8 %collective-permute-start.2 = (f32[1024,1,128]{2,0,1:T(8,128)}, f32[1024,1,128]{2,0,1:T(8,128)}, u32[]{:S(2)}, u32[]{:S(2)}) collective-permute-start(f32[1024,1,128]{2,0,1:T(8,128)} %maximum_add_fusion.7), channel_id=1, source_target_pairs={{15,0},{0,1},{1,2},{2,3},{3,4},{4,5},{5,6},{6,7},{7,8},{8,9},{9,10... | collective-permute-start | bytes 1572872 | tf_op jit(solution)/shard_map/while/body/eval_jaxpr/ppermute | solution.py:14
  98.5 21.8 %collective-permute-start.3 = (f32[1024,1,128]{2,0,1:T(8,128)}, f32[1024,1,128]{2,0,1:T(8,128)}, u32[]{:S(2)}, u32[]{:S(2)}) collective-permute-start(f32[1024,1,128]{2,0,1:T(8,128)} %maximum_add_fusion.8), channel_id=1, source_target_pairs={{15,0},{0,1},{1,2},{2,3},{3,4},{4,5},{5,6},{6,7},{7,8},{8,9},{9,10... | collective-permute-start | bytes 1572872 | tf_op jit(solution)/shard_map/while/body/eval_jaxpr/ppermute | solution.py:14
  142.9 23.8 %collective-permute-start.2 = (f32[1024,1,128]{2,0,1:T(8,128)}, f32[1024,1,128]{2,0,1:T(8,128)}, u32[]{:S(2)}, u32[]{:S(2)}) collective-permute-start(f32[1024,1,128]{2,0,1:T(8,128)} %maximum_add_fusion.7), channel_id=1, source_target_pairs={{15,0},{0,1},{1,2},{2,3},{3,4},{4,5},{5,6},{6,7},{7,8},{8,9},{9,10... | collective-permute-start | bytes 1572872 | tf_op jit(solution)/shard_map/while/body/eval_jaxpr/ppermute | solution.py:14
  144.9 21.8 %collective-permute-start.3 = (f32[1024,1,128]{2,0,1:T(8,128)}, f32[1024,1,128]{2,0,1:T(8,128)}, u32[]{:S(2)}, u32[]{:S(2)}) collective-permute-start(f32[1024,1,128]{2,0,1:T(8,128)} %maximum_add_fusion.8), channel_id=1, source_target_pairs={{15,0},{0,1},{1,2},{2,3},{3,4},{4,5},{5,6},{6,7},{7,8},{8,9},{9,10... | collective-permute-start | bytes 1572872 | tf_op jit(solution)/shard_map/while/body/eval_jaxpr/ppermute | solution.py:14
  145.6 21.1 %collective-permute-start.1 = (bf16[1024,1,128]{2,0,1:T(8,128)(2,1)S(1)}, bf16[1024,1,128]{2,0,1:T(8,128)(2,1)}, u32[]{:S(2)}, u32[]{:S(2)}) collective-permute-start(bf16[1024,1,128]{2,0,1:T(8,128)(2,1)S(1)} %copy.173), channel_id=1, source_target_pairs={{15,0},{0,1},{1,2},{2,3},{3,4},{4,5},{5,6},{6,7},{7,8},{8,9},{9,10... | collective-permute-start | bytes 786440 | tf_op jit(solution)/shard_map/while/body/eval_jaxpr/ppermute | solution.py:14
  189.2 23.8 %collective-permute-start.2 = (f32[1024,1,128]{2,0,1:T(8,128)}, f32[1024,1,128]{2,0,1:T(8,128)}, u32[]{:S(2)}, u32[]{:S(2)}) collective-permute-start(f32[1024,1,128]{2,0,1:T(8,128)} %maximum_add_fusion.7), channel_id=1, source_target_pairs={{15,0},{0,1},{1,2},{2,3},{3,4},{4,5},{5,6},{6,7},{7,8},{8,9},{9,10... | collective-permute-start | bytes 1572872 | tf_op jit(solution)/shard_map/while/body/eval_jaxpr/ppermute | solution.py:14
  191.2 21.8 %collective-permute-start.3 = (f32[1024,1,128]{2,0,1:T(8,128)}, f32[1024,1,128]{2,0,1:T(8,128)}, u32[]{:S(2)}, u32[]{:S(2)}) collective-permute-start(f32[1024,1,128]{2,0,1:T(8,128)} %maximum_add_fusion.8), channel_id=1, source_target_pairs={{15,0},{0,1},{1,2},{2,3},{3,4},{4,5},{5,6},{6,7},{7,8},{8,9},{9,10... | collective-permute-start | bytes 1572872 | tf_op jit(solution)/shard_map/while/body/eval_jaxpr/ppermute | solution.py:14
  191.2 19.0 %collective-permute-start = (bf16[1024,1,128]{2,0,1:T(8,128)(2,1)S(1)}, bf16[1024,1,128]{2,0,1:T(8,128)(2,1)}, u32[]{:S(2)}, u32[]{:S(2)}) collective-permute-start(bf16[1024,1,128]{2,0,1:T(8,128)(2,1)S(1)} %copy.172), channel_id=1, source_target_pairs={{15,0},{0,1},{1,2},{2,3},{3,4},{4,5},{5,6},{6,7},{7,8},{8,9},{9,10... | collective-permute-start | bytes 786440 | tf_op jit(solution)/shard_map/while/body/eval_jaxpr/ppermute | solution.py:14
  191.2 21.8 %collective-permute-start.1 = (bf16[1024,1,128]{2,0,1:T(8,128)(2,1)S(1)}, bf16[1024,1,128]{2,0,1:T(8,128)(2,1)}, u32[]{:S(2)}, u32[]{:S(2)}) collective-permute-start(bf16[1024,1,128]{2,0,1:T(8,128)(2,1)S(1)} %copy.173), channel_id=1, source_target_pairs={{15,0},{0,1},{1,2},{2,3},{3,4},{4,5},{5,6},{6,7},{7,8},{8,9},{9,10... | collective-permute-start | bytes 786440 | tf_op jit(solution)/shard_map/while/body/eval_jaxpr/ppermute | solution.py:14
  235.6 23.8 %collective-permute-start.2 = (f32[1024,1,128]{2,0,1:T(8,128)}, f32[1024,1,128]{2,0,1:T(8,128)}, u32[]{:S(2)}, u32[]{:S(2)}) collective-permute-start(f32[1024,1,128]{2,0,1:T(8,128)} %maximum_add_fusion.7), channel_id=1, source_target_pairs={{15,0},{0,1},{1,2},{2,3},{3,4},{4,5},{5,6},{6,7},{7,8},{8,9},{9,10... | collective-permute-start | bytes 1572872 | tf_op jit(solution)/shard_map/while/body/eval_jaxpr/ppermute | solution.py:14
  237.6 21.8 %collective-permute-start.3 = (f32[1024,1,128]{2,0,1:T(8,128)}, f32[1024,1,128]{2,0,1:T(8,128)}, u32[]{:S(2)}, u32[]{:S(2)}) collective-permute-start(f32[1024,1,128]{2,0,1:T(8,128)} %maximum_add_fusion.8), channel_id=1, source_target_pairs={{15,0},{0,1},{1,2},{2,3},{3,4},{4,5},{5,6},{6,7},{7,8},{8,9},{9,10... | collective-permute-start | bytes 1572872 | tf_op jit(solution)/shard_map/while/body/eval_jaxpr/ppermute | solution.py:14
  237.6 21.8 %collective-permute-start.1 = (bf16[1024,1,128]{2,0,1:T(8,128)(2,1)S(1)}, bf16[1024,1,128]{2,0,1:T(8,128)(2,1)}, u32[]{:S(2)}, u32[]{:S(2)}) collective-permute-start(bf16[1024,1,128]{2,0,1:T(8,128)(2,1)S(1)} %copy.173), channel_id=1, source_target_pairs={{15,0},{0,1},{1,2},{2,3},{3,4},{4,5},{5,6},{6,7},{7,8},{8,9},{9,10... | collective-permute-start | bytes 786440 | tf_op jit(solution)/shard_map/while/body/eval_jaxpr/ppermute | solution.py:14
  281.9 23.8 %collective-permute-start.2 = (f32[1024,1,128]{2,0,1:T(8,128)}, f32[1024,1,128]{2,0,1:T(8,128)}, u32[]{:S(2)}, u32[]{:S(2)}) collective-permute-start(f32[1024,1,128]{2,0,1:T(8,128)} %maximum_add_fusion.7), channel_id=1, source_target_pairs={{15,0},{0,1},{1,2},{2,3},{3,4},{4,5},{5,6},{6,7},{7,8},{8,9},{9,10... | collective-permute-start | bytes 1572872 | tf_op jit(solution)/shard_map/while/body/eval_jaxpr/ppermute | solution.py:14
  283.9 21.8 %collective-permute-start.3 = (f32[1024,1,128]{2,0,1:T(8,128)}, f32[1024,1,128]{2,0,1:T(8,128)}, u32[]{:S(2)}, u32[]{:S(2)}) collective-permute-start(f32[1024,1,128]{2,0,1:T(8,128)} %maximum_add_fusion.8), channel_id=1, source_target_pairs={{15,0},{0,1},{1,2},{2,3},{3,4},{4,5},{5,6},{6,7},{7,8},{8,9},{9,10... | collective-permute-start | bytes 1572872 | tf_op jit(solution)/shard_map/while/body/eval_jaxpr/ppermute | solution.py:14
  283.9 21.8 %collective-permute-start.1 = (bf16[1024,1,128]{2,0,1:T(8,128)(2,1)S(1)}, bf16[1024,1,128]{2,0,1:T(8,128)(2,1)}, u32[]{:S(2)}, u32[]{:S(2)}) collective-permute-start(bf16[1024,1,128]{2,0,1:T(8,128)(2,1)S(1)} %copy.173), channel_id=1, source_target_pairs={{15,0},{0,1},{1,2},{2,3},{3,4},{4,5},{5,6},{6,7},{7,8},{8,9},{9,10... | collective-permute-start | bytes 786440 | tf_op jit(solution)/shard_map/while/body/eval_jaxpr/ppermute | solution.py:14
  328.3 23.8 %collective-permute-start.2 = (f32[1024,1,128]{2,0,1:T(8,128)}, f32[1024,1,128]{2,0,1:T(8,128)}, u32[]{:S(2)}, u32[]{:S(2)}) collective-permute-start(f32[1024,1,128]{2,0,1:T(8,128)} %maximum_add_fusion.7), channel_id=1, source_target_pairs={{15,0},{0,1},{1,2},{2,3},{3,4},{4,5},{5,6},{6,7},{7,8},{8,9},{9,10... | collective-permute-start | bytes 1572872 | tf_op jit(solution)/shard_map/while/body/eval_jaxpr/ppermute | solution.py:14
  330.2 21.8 %collective-permute-start.3 = (f32[1024,1,128]{2,0,1:T(8,128)}, f32[1024,1,128]{2,0,1:T(8,128)}, u32[]{:S(2)}, u32[]{:S(2)}) collective-permute-start(f32[1024,1,128]{2,0,1:T(8,128)} %maximum_add_fusion.8), channel_id=1, source_target_pairs={{15,0},{0,1},{1,2},{2,3},{3,4},{4,5},{5,6},{6,7},{7,8},{8,9},{9,10... | collective-permute-start | bytes 1572872 | tf_op jit(solution)/shard_map/while/body/eval_jaxpr/ppermute | solution.py:14
  330.3 21.8 %collective-permute-start.1 = (bf16[1024,1,128]{2,0,1:T(8,128)(2,1)S(1)}, bf16[1024,1,128]{2,0,1:T(8,128)(2,1)}, u32[]{:S(2)}, u32[]{:S(2)}) collective-permute-start(bf16[1024,1,128]{2,0,1:T(8,128)(2,1)S(1)} %copy.173), channel_id=1, source_target_pairs={{15,0},{0,1},{1,2},{2,3},{3,4},{4,5},{5,6},{6,7},{7,8},{8,9},{9,10... | collective-permute-start | bytes 786440 | tf_op jit(solution)/shard_map/while/body/eval_jaxpr/ppermute | solution.py:14
  374.6 23.8 %collective-permute-start.2 = (f32[1024,1,128]{2,0,1:T(8,128)}, f32[1024,1,128]{2,0,1:T(8,128)}, u32[]{:S(2)}, u32[]{:S(2)}) collective-permute-start(f32[1024,1,128]{2,0,1:T(8,128)} %maximum_add_fusion.7), channel_id=1, source_target_pairs={{15,0},{0,1},{1,2},{2,3},{3,4},{4,5},{5,6},{6,7},{7,8},{8,9},{9,10... | collective-permute-start | bytes 1572872 | tf_op jit(solution)/shard_map/while/body/eval_jaxpr/ppermute | solution.py:14
  376.6 21.8 %collective-permute-start.3 = (f32[1024,1,128]{2,0,1:T(8,128)}, f32[1024,1,128]{2,0,1:T(8,128)}, u32[]{:S(2)}, u32[]{:S(2)}) collective-permute-start(f32[1024,1,128]{2,0,1:T(8,128)} %maximum_add_fusion.8), channel_id=1, source_target_pairs={{15,0},{0,1},{1,2},{2,3},{3,4},{4,5},{5,6},{6,7},{7,8},{8,9},{9,10... | collective-permute-start | bytes 1572872 | tf_op jit(solution)/shard_map/while/body/eval_jaxpr/ppermute | solution.py:14
  376.6 21.8 %collective-permute-start.1 = (bf16[1024,1,128]{2,0,1:T(8,128)(2,1)S(1)}, bf16[1024,1,128]{2,0,1:T(8,128)(2,1)}, u32[]{:S(2)}, u32[]{:S(2)}) collective-permute-start(bf16[1024,1,128]{2,0,1:T(8,128)(2,1)S(1)} %copy.173), channel_id=1, source_target_pairs={{15,0},{0,1},{1,2},{2,3},{3,4},{4,5},{5,6},{6,7},{7,8},{8,9},{9,10... | collective-permute-start | bytes 786440 | tf_op jit(solution)/shard_map/while/body/eval_jaxpr/ppermute | solution.py:14
  421.0 23.8 %collective-permute-start.2 = (f32[1024,1,128]{2,0,1:T(8,128)}, f32[1024,1,128]{2,0,1:T(8,128)}, u32[]{:S(2)}, u32[]{:S(2)}) collective-permute-start(f32[1024,1,128]{2,0,1:T(8,128)} %maximum_add_fusion.7), channel_id=1, source_target_pairs={{15,0},{0,1},{1,2},{2,3},{3,4},{4,5},{5,6},{6,7},{7,8},{8,9},{9,10... | collective-permute-start | bytes 1572872 | tf_op jit(solution)/shard_map/while/body/eval_jaxpr/ppermute | solution.py:14
  422.9 21.8 %collective-permute-start.3 = (f32[1024,1,128]{2,0,1:T(8,128)}, f32[1024,1,128]{2,0,1:T(8,128)}, u32[]{:S(2)}, u32[]{:S(2)}) collective-permute-start(f32[1024,1,128]{2,0,1:T(8,128)} %maximum_add_fusion.8), channel_id=1, source_target_pairs={{15,0},{0,1},{1,2},{2,3},{3,4},{4,5},{5,6},{6,7},{7,8},{8,9},{9,10... | collective-permute-start | bytes 1572872 | tf_op jit(solution)/shard_map/while/body/eval_jaxpr/ppermute | solution.py:14
  422.9 21.8 %collective-permute-start.1 = (bf16[1024,1,128]{2,0,1:T(8,128)(2,1)S(1)}, bf16[1024,1,128]{2,0,1:T(8,128)(2,1)}, u32[]{:S(2)}, u32[]{:S(2)}) collective-permute-start(bf16[1024,1,128]{2,0,1:T(8,128)(2,1)S(1)} %copy.173), channel_id=1, source_target_pairs={{15,0},{0,1},{1,2},{2,3},{3,4},{4,5},{5,6},{6,7},{7,8},{8,9},{9,10... | collective-permute-start | bytes 786440 | tf_op jit(solution)/shard_map/while/body/eval_jaxpr/ppermute | solution.py:14
  467.3 23.8 %collective-permute-start.2 = (f32[1024,1,128]{2,0,1:T(8,128)}, f32[1024,1,128]{2,0,1:T(8,128)}, u32[]{:S(2)}, u32[]{:S(2)}) collective-permute-start(f32[1024,1,128]{2,0,1:T(8,128)} %maximum_add_fusion.7), channel_id=1, source_target_pairs={{15,0},{0,1},{1,2},{2,3},{3,4},{4,5},{5,6},{6,7},{7,8},{8,9},{9,10... | collective-permute-start | bytes 1572872 | tf_op jit(solution)/shard_map/while/body/eval_jaxpr/ppermute | solution.py:14
  469.3 21.8 %collective-permute-start.3 = (f32[1024,1,128]{2,0,1:T(8,128)}, f32[1024,1,128]{2,0,1:T(8,128)}, u32[]{:S(2)}, u32[]{:S(2)}) collective-permute-start(f32[1024,1,128]{2,0,1:T(8,128)} %maximum_add_fusion.8), channel_id=1, source_target_pairs={{15,0},{0,1},{1,2},{2,3},{3,4},{4,5},{5,6},{6,7},{7,8},{8,9},{9,10... | collective-permute-start | bytes 1572872 | tf_op jit(solution)/shard_map/while/body/eval_jaxpr/ppermute | solution.py:14
  469.3 21.8 %collective-permute-start.1 = (bf16[1024,1,128]{2,0,1:T(8,128)(2,1)S(1)}, bf16[1024,1,128]{2,0,1:T(8,128)(2,1)}, u32[]{:S(2)}, u32[]{:S(2)}) collective-permute-start(bf16[1024,1,128]{2,0,1:T(8,128)(2,1)S(1)} %copy.173), channel_id=1, source_target_pairs={{15,0},{0,1},{1,2},{2,3},{3,4},{4,5},{5,6},{6,7},{7,8},{8,9},{9,10... | collective-permute-start | bytes 786440 | tf_op jit(solution)/shard_map/while/body/eval_jaxpr/ppermute | solution.py:14
  513.6 23.8 %collective-permute-start.2 = (f32[1024,1,128]{2,0,1:T(8,128)}, f32[1024,1,128]{2,0,1:T(8,128)}, u32[]{:S(2)}, u32[]{:S(2)}) collective-permute-start(f32[1024,1,128]{2,0,1:T(8,128)} %maximum_add_fusion.7), channel_id=1, source_target_pairs={{15,0},{0,1},{1,2},{2,3},{3,4},{4,5},{5,6},{6,7},{7,8},{8,9},{9,10... | collective-permute-start | bytes 1572872 | tf_op jit(solution)/shard_map/while/body/eval_jaxpr/ppermute | solution.py:14
  515.6 21.8 %collective-permute-start.3 = (f32[1024,1,128]{2,0,1:T(8,128)}, f32[1024,1,128]{2,0,1:T(8,128)}, u32[]{:S(2)}, u32[]{:S(2)}) collective-permute-start(f32[1024,1,128]{2,0,1:T(8,128)} %maximum_add_fusion.8), channel_id=1, source_target_pairs={{15,0},{0,1},{1,2},{2,3},{3,4},{4,5},{5,6},{6,7},{7,8},{8,9},{9,10... | collective-permute-start | bytes 1572872 | tf_op jit(solution)/shard_map/while/body/eval_jaxpr/ppermute | solution.py:14
  515.6 21.8 %collective-permute-start.1 = (bf16[1024,1,128]{2,0,1:T(8,128)(2,1)S(1)}, bf16[1024,1,128]{2,0,1:T(8,128)(2,1)}, u32[]{:S(2)}, u32[]{:S(2)}) collective-permute-start(bf16[1024,1,128]{2,0,1:T(8,128)(2,1)S(1)} %copy.173), channel_id=1, source_target_pairs={{15,0},{0,1},{1,2},{2,3},{3,4},{4,5},{5,6},{6,7},{7,8},{8,9},{9,10... | collective-permute-start | bytes 786440 | tf_op jit(solution)/shard_map/while/body/eval_jaxpr/ppermute | solution.py:14
  560.0 23.8 %collective-permute-start.2 = (f32[1024,1,128]{2,0,1:T(8,128)}, f32[1024,1,128]{2,0,1:T(8,128)}, u32[]{:S(2)}, u32[]{:S(2)}) collective-permute-start(f32[1024,1,128]{2,0,1:T(8,128)} %maximum_add_fusion.7), channel_id=1, source_target_pairs={{15,0},{0,1},{1,2},{2,3},{3,4},{4,5},{5,6},{6,7},{7,8},{8,9},{9,10... | collective-permute-start | bytes 1572872 | tf_op jit(solution)/shard_map/while/body/eval_jaxpr/ppermute | solution.py:14
  562.0 21.8 %collective-permute-start.3 = (f32[1024,1,128]{2,0,1:T(8,128)}, f32[1024,1,128]{2,0,1:T(8,128)}, u32[]{:S(2)}, u32[]{:S(2)}) collective-permute-start(f32[1024,1,128]{2,0,1:T(8,128)} %maximum_add_fusion.8), channel_id=1, source_target_pairs={{15,0},{0,1},{1,2},{2,3},{3,4},{4,5},{5,6},{6,7},{7,8},{8,9},{9,10... | collective-permute-start | bytes 1572872 | tf_op jit(solution)/shard_map/while/body/eval_jaxpr/ppermute | solution.py:14
  562.0 21.8 %collective-permute-start.1 = (bf16[1024,1,128]{2,0,1:T(8,128)(2,1)S(1)}, bf16[1024,1,128]{2,0,1:T(8,128)(2,1)}, u32[]{:S(2)}, u32[]{:S(2)}) collective-permute-start(bf16[1024,1,128]{2,0,1:T(8,128)(2,1)S(1)} %copy.173), channel_id=1, source_target_pairs={{15,0},{0,1},{1,2},{2,3},{3,4},{4,5},{5,6},{6,7},{7,8},{8,9},{9,10... | collective-permute-start | bytes 786440 | tf_op jit(solution)/shard_map/while/body/eval_jaxpr/ppermute | solution.py:14
  606.3 23.8 %collective-permute-start.2 = (f32[1024,1,128]{2,0,1:T(8,128)}, f32[1024,1,128]{2,0,1:T(8,128)}, u32[]{:S(2)}, u32[]{:S(2)}) collective-permute-start(f32[1024,1,128]{2,0,1:T(8,128)} %maximum_add_fusion.7), channel_id=1, source_target_pairs={{15,0},{0,1},{1,2},{2,3},{3,4},{4,5},{5,6},{6,7},{7,8},{8,9},{9,10... | collective-permute-start | bytes 1572872 | tf_op jit(solution)/shard_map/while/body/eval_jaxpr/ppermute | solution.py:14
  608.3 21.8 %collective-permute-start.3 = (f32[1024,1,128]{2,0,1:T(8,128)}, f32[1024,1,128]{2,0,1:T(8,128)}, u32[]{:S(2)}, u32[]{:S(2)}) collective-permute-start(f32[1024,1,128]{2,0,1:T(8,128)} %maximum_add_fusion.8), channel_id=1, source_target_pairs={{15,0},{0,1},{1,2},{2,3},{3,4},{4,5},{5,6},{6,7},{7,8},{8,9},{9,10... | collective-permute-start | bytes 1572872 | tf_op jit(solution)/shard_map/while/body/eval_jaxpr/ppermute | solution.py:14
  608.3 21.8 %collective-permute-start.1 = (bf16[1024,1,128]{2,0,1:T(8,128)(2,1)S(1)}, bf16[1024,1,128]{2,0,1:T(8,128)(2,1)}, u32[]{:S(2)}, u32[]{:S(2)}) collective-permute-start(bf16[1024,1,128]{2,0,1:T(8,128)(2,1)S(1)} %copy.173), channel_id=1, source_target_pairs={{15,0},{0,1},{1,2},{2,3},{3,4},{4,5},{5,6},{6,7},{7,8},{8,9},{9,10... | collective-permute-start | bytes 786440 | tf_op jit(solution)/shard_map/while/body/eval_jaxpr/ppermute | solution.py:14
  652.7 23.8 %collective-permute-start.2 = (f32[1024,1,128]{2,0,1:T(8,128)}, f32[1024,1,128]{2,0,1:T(8,128)}, u32[]{:S(2)}, u32[]{:S(2)}) collective-permute-start(f32[1024,1,128]{2,0,1:T(8,128)} %maximum_add_fusion.7), channel_id=1, source_target_pairs={{15,0},{0,1},{1,2},{2,3},{3,4},{4,5},{5,6},{6,7},{7,8},{8,9},{9,10... | collective-permute-start | bytes 1572872 | tf_op jit(solution)/shard_map/while/body/eval_jaxpr/ppermute | solution.py:14
  654.6 21.8 %collective-permute-start.3 = (f32[1024,1,128]{2,0,1:T(8,128)}, f32[1024,1,128]{2,0,1:T(8,128)}, u32[]{:S(2)}, u32[]{:S(2)}) collective-permute-start(f32[1024,1,128]{2,0,1:T(8,128)} %maximum_add_fusion.8), channel_id=1, source_target_pairs={{15,0},{0,1},{1,2},{2,3},{3,4},{4,5},{5,6},{6,7},{7,8},{8,9},{9,10... | collective-permute-start | bytes 1572872 | tf_op jit(solution)/shard_map/while/body/eval_jaxpr/ppermute | solution.py:14
  654.6 21.8 %collective-permute-start.1 = (bf16[1024,1,128]{2,0,1:T(8,128)(2,1)S(1)}, bf16[1024,1,128]{2,0,1:T(8,128)(2,1)}, u32[]{:S(2)}, u32[]{:S(2)}) collective-permute-start(bf16[1024,1,128]{2,0,1:T(8,128)(2,1)S(1)} %copy.173), channel_id=1, source_target_pairs={{15,0},{0,1},{1,2},{2,3},{3,4},{4,5},{5,6},{6,7},{7,8},{8,9},{9,10... | collective-permute-start | bytes 786440 | tf_op jit(solution)/shard_map/while/body/eval_jaxpr/ppermute | solution.py:14
  699.0 23.8 %collective-permute-start.2 = (f32[1024,1,128]{2,0,1:T(8,128)}, f32[1024,1,128]{2,0,1:T(8,128)}, u32[]{:S(2)}, u32[]{:S(2)}) collective-permute-start(f32[1024,1,128]{2,0,1:T(8,128)} %maximum_add_fusion.7), channel_id=1, source_target_pairs={{15,0},{0,1},{1,2},{2,3},{3,4},{4,5},{5,6},{6,7},{7,8},{8,9},{9,10... | collective-permute-start | bytes 1572872 | tf_op jit(solution)/shard_map/while/body/eval_jaxpr/ppermute | solution.py:14
  701.0 21.8 %collective-permute-start.3 = (f32[1024,1,128]{2,0,1:T(8,128)}, f32[1024,1,128]{2,0,1:T(8,128)}, u32[]{:S(2)}, u32[]{:S(2)}) collective-permute-start(f32[1024,1,128]{2,0,1:T(8,128)} %maximum_add_fusion.8), channel_id=1, source_target_pairs={{15,0},{0,1},{1,2},{2,3},{3,4},{4,5},{5,6},{6,7},{7,8},{8,9},{9,10... | collective-permute-start | bytes 1572872 | tf_op jit(solution)/shard_map/while/body/eval_jaxpr/ppermute | solution.py:14
  701.0 21.8 %collective-permute-start.1 = (bf16[1024,1,128]{2,0,1:T(8,128)(2,1)S(1)}, bf16[1024,1,128]{2,0,1:T(8,128)(2,1)}, u32[]{:S(2)}, u32[]{:S(2)}) collective-permute-start(bf16[1024,1,128]{2,0,1:T(8,128)(2,1)S(1)} %copy.173), channel_id=1, source_target_pairs={{15,0},{0,1},{1,2},{2,3},{3,4},{4,5},{5,6},{6,7},{7,8},{8,9},{9,10... | collective-permute-start | bytes 786440 | tf_op jit(solution)/shard_map/while/body/eval_jaxpr/ppermute | solution.py:14
  745.3 23.8 %collective-permute-start.2 = (f32[1024,1,128]{2,0,1:T(8,128)}, f32[1024,1,128]{2,0,1:T(8,128)}, u32[]{:S(2)}, u32[]{:S(2)}) collective-permute-start(f32[1024,1,128]{2,0,1:T(8,128)} %maximum_add_fusion.7), channel_id=1, source_target_pairs={{15,0},{0,1},{1,2},{2,3},{3,4},{4,5},{5,6},{6,7},{7,8},{8,9},{9,10... | collective-permute-start | bytes 1572872 | tf_op jit(solution)/shard_map/while/body/eval_jaxpr/ppermute | solution.py:14
  747.3 21.8 %collective-permute-start.3 = (f32[1024,1,128]{2,0,1:T(8,128)}, f32[1024,1,128]{2,0,1:T(8,128)}, u32[]{:S(2)}, u32[]{:S(2)}) collective-permute-start(f32[1024,1,128]{2,0,1:T(8,128)} %maximum_add_fusion.8), channel_id=1, source_target_pairs={{15,0},{0,1},{1,2},{2,3},{3,4},{4,5},{5,6},{6,7},{7,8},{8,9},{9,10... | collective-permute-start | bytes 1572872 | tf_op jit(solution)/shard_map/while/body/eval_jaxpr/ppermute | solution.py:14
  747.3 21.8 %collective-permute-start.1 = (bf16[1024,1,128]{2,0,1:T(8,128)(2,1)S(1)}, bf16[1024,1,128]{2,0,1:T(8,128)(2,1)}, u32[]{:S(2)}, u32[]{:S(2)}) collective-permute-start(bf16[1024,1,128]{2,0,1:T(8,128)(2,1)S(1)} %copy.173), channel_id=1, source_target_pairs={{15,0},{0,1},{1,2},{2,3},{3,4},{4,5},{5,6},{6,7},{7,8},{8,9},{9,10... | collective-permute-start | bytes 786440 | tf_op jit(solution)/shard_map/while/body/eval_jaxpr/ppermute | solution.py:14
  791.7 23.8 %collective-permute-start.2 = (f32[1024,1,128]{2,0,1:T(8,128)}, f32[1024,1,128]{2,0,1:T(8,128)}, u32[]{:S(2)}, u32[]{:S(2)}) collective-permute-start(f32[1024,1,128]{2,0,1:T(8,128)} %maximum_add_fusion.7), channel_id=1, source_target_pairs={{15,0},{0,1},{1,2},{2,3},{3,4},{4,5},{5,6},{6,7},{7,8},{8,9},{9,10... | collective-permute-start | bytes 1572872 | tf_op jit(solution)/shard_map/while/body/eval_jaxpr/ppermute | solution.py:14
  793.7 21.8 %collective-permute-start.3 = (f32[1024,1,128]{2,0,1:T(8,128)}, f32[1024,1,128]{2,0,1:T(8,128)}, u32[]{:S(2)}, u32[]{:S(2)}) collective-permute-start(f32[1024,1,128]{2,0,1:T(8,128)} %maximum_add_fusion.8), channel_id=1, source_target_pairs={{15,0},{0,1},{1,2},{2,3},{3,4},{4,5},{5,6},{6,7},{7,8},{8,9},{9,10... | collective-permute-start | bytes 1572872 | tf_op jit(solution)/shard_map/while/body/eval_jaxpr/ppermute | solution.py:14
  793.7 21.8 %collective-permute-start.1 = (bf16[1024,1,128]{2,0,1:T(8,128)(2,1)S(1)}, bf16[1024,1,128]{2,0,1:T(8,128)(2,1)}, u32[]{:S(2)}, u32[]{:S(2)}) collective-permute-start(bf16[1024,1,128]{2,0,1:T(8,128)(2,1)S(1)} %copy.173), channel_id=1, source_target_pairs={{15,0},{0,1},{1,2},{2,3},{3,4},{4,5},{5,6},{6,7},{7,8},{8,9},{9,10... | collective-permute-start | bytes 786440 | tf_op jit(solution)/shard_map/while/body/eval_jaxpr/ppermute | solution.py:14
  (124 other events, 731.0 us)
where the time goes:
time: 861 us; the launch traced here: 854 us
  waiting for transfers between devices  322 us (37%)
  other arithmetic  179 us (21%)
  loops' own time  109 us (13%)
  local copies, waits for them, and re-layouts  97.4 us (11%)
  matrix products  87.7 us (10%)
  starting transfers between devices  46.2 us (5%)
  blocking collectives  11.2 us (1%)
    ppermute x64, waiting for transfers between devices, from_behind(): return lax.ppermute(block, axis, route)  281 us
    another operation x1, loops' own time, per_device(): finished = lax.fori_loop(0, group_count, joined_turn, initial)  107 us
    while x224, local copies, waits for them, and re-layouts  52.9 us
    add x32, other arithmetic, contribute(): key_halves[key_side] = key_halves[key_side] + found[1]  47.4 us
    add x16, other arithmetic, absorb(): query_acc + query_part  36.2 us
    add x16, other arithmetic, absorb(): key_gradient_total + key_part  31.4 us
    add x16, other arithmetic, absorb(): value_gradient_total + value_part  30.2 us
    dot_general x33, matrix products, attend(): jnp.einsum('qhgd,khd->hgqk', query_groups, key_row_block, preferred_eleme...  22.5 us
  transfers between devices with their start and end apart: 72, of which 40 were waited for; matrix products, arithmetic and copies ran while one was open for 12% of the time, Pallas kernels for 0%

commit v1 on v0

v1 whole, which is shorter than its diff:
```python
import functools

import jax
import jax.numpy as jnp
from jax import lax
from jax.experimental import pallas as pl
from jax.experimental.pallas import tpu as pltpu
from jax.sharding import PartitionSpec as P

MESH = pl.DeviceIdType.MESH
F32, BF16 = jnp.float32, jnp.bfloat16
HEAD = 128
HEADS = 8
PART = 128
HALF = 512
ROWS = 1024
LOG2E = 1.4426950408889634
SCALE = HEAD**-0.5
TILE = 256
NT = (((1,), (1,)), ((), ()))


def remote(src, dst, send_sem, recv_sem, device):
    return pltpu.make_async_remote_copy(
        src_ref=src,
        dst_ref=dst,
        send_sem=send_sem,
        recv_sem=recv_sem,
        device_id=device,
        device_id_type=MESH,
    )


def dot(a, b):
    return jnp.dot(a, b, preferred_element_type=F32)


def dot_nt(a, b):
    return lax.dot_general(a, b, NT, preferred_element_type=F32)


def block(q, do, stats, k, v, mask):
    k_t = k.T
    dk = dv = None
    dq = []
    for e in range(2):
        for t in range(HALF // TILE):
            cols = slice(t * TILE, (t + 1) * TILE)
            q_e = q[cols, e * HEAD : (e + 1) * HEAD]
            do_e = do[cols, e * HEAD : (e + 1) * HEAD]
            scores = dot_nt(k, q_e)
            probs = jnp.exp2(scores * (SCALE * LOG2E) - stats[e : e + 1, cols])
            if mask:
                key_id = lax.broadcasted_iota(jnp.int32, (HALF, TILE), 0)
                query_id = lax.broadcasted_iota(jnp.int32, (HALF, TILE), 1) + t * TILE
                probs = jnp.where(key_id <= query_id, probs, 0.0)
            prob_grad = dot_nt(v, do_e)
            score_grad = (probs * (prob_grad - stats[2 + e : 3 + e, cols])).astype(BF16)
            dv_e = dot(probs.astype(BF16), do_e)
            dk_e = dot(score_grad, q_e)
            dv = dv_e if dv is None else dv + dv_e
            dk = dk_e if dk is None else dk + dk_e
            dq.append((e, t, dot(k_t, score_grad)))
    return dq, dk, dv


def kernel(
    order,
    q_in,
    k_in,
    v_in,
    o_in,
    do_in,
    lse_in,
    dq_out,
    dk_out,
    dv_out,
    o_vm,
    do_vm,
    stat_send,
    QD,
    KV,
    ST,
    DQ,
    DKV,
    dq_send,
    dq_recv,
    core_recv,
    far_send,
    far_recv,
    dq_fin,
    dkv_fin,
    s_loc,
    s_a2a,
    r_a2a,
    s_q,
    r_q,
    s_k,
    r_k,
    s_dq,
    r_dq,
    s_dk,
    r_dk,
    s_out,
    r_out,
):
    head, inner, outer = lax.axis_index("head"), lax.axis_index("inner"), lax.axis_index("outer")
    x_lo, z = head // 4, head % 4
    x_hi, core = outer // 2, outer % 2

    def peer(r):
        return ((x_lo + r // 4) % 2) * 4 + (z + r % 4) % 4

    q_dev = {
        1: (head, (inner + 1) % 4, outer),
        2: (head, (inner + 3) % 4, outer),
        3: (head, (inner + 2) % 4, outer),
    }
    back_dev = {1: q_dev[2], 2: q_dev[1], 3: q_dev[3]}
    core_dev = (head, inner, x_hi * 2 + (core + 1) % 2)
    far_dev = (head, inner, ((x_hi + 1) % 2) * 2 + core)

    barrier = pltpu.get_barrier_semaphore()
    everyone = [(peer(r), inner, outer) for r in range(1, 8)] + [q_dev[1], q_dev[2], q_dev[3], core_dev, far_dev]
    for device in everyone:
        pl.semaphore_signal(barrier, inc=1, device_id=device, device_id_type=MESH)

    mine = pl.ds(pl.multiple_of(head * PART, PART), PART)

    def wide(p, n):
        return pl.ds(pl.multiple_of(p * n, n), n)

    local = [
        pltpu.make_async_copy(o_in.at[0], o_vm, s_loc.at[0]),
        pltpu.make_async_copy(do_in.at[0], do_vm, s_loc.at[1]),
        pltpu.make_async_copy(q_in.at[0, :, wide(head, 256)], QD.at[0, 0, mine], s_loc.at[2]),
        pltpu.make_async_copy(do_in.at[0, :, wide(head, 256)], QD.at[0, 1, mine], s_loc.at[3]),
        pltpu.make_async_copy(k_in.at[0, :, wide(head, 128)], KV.at[0, 0, mine], s_loc.at[4]),
        pltpu.make_async_copy(v_in.at[0, :, wide(head, 128)], KV.at[0, 1, mine], s_loc.at[5]),
    ]
    for copy in local:
        copy.start()
    pl.semaphore_wait(barrier, len(everyone))

    def exchange(i, r):
        p = peer(r)
        src, dst = [
            (k_in.at[0, :, wide(p, 128)], KV.at[0, 0, mine]),
            (v_in.at[0, :, wide(p, 128)], KV.at[0, 1, mine]),
            (q_in.at[0, :, wide(p, 256)], QD.at[0, 0, mine]),
            (do_in.at[0, :, wide(p, 256)], QD.at[0, 1, mine]),
            (stat_send.at[p], ST.at[0, :, mine]),
        ][i]
        return remote(src, dst, s_a2a.at[i, r], r_a2a.at[i, r], (p, inner, outer))

    for r in range(1, 8):
        for i in range(4):
            exchange(i, r).start()

    local[0].wait()
    local[1].wait()
    lane = lax.broadcasted_iota(jnp.int32, (PART, 128), 1)
    delta = jnp.zeros((PART, 128), F32)
    for h in range(2 * HEADS):
        cols = slice(h * HEAD, (h + 1) * HEAD)
        total = jnp.sum(o_vm[:, cols].astype(F32) * do_vm[:, cols].astype(F32), axis=1, keepdims=True)
        delta = jnp.where(lane == h, total, delta)
    delta_t = delta.T
    lse_t = (lse_in[0] * LOG2E).T
    stat_send[...] = jnp.zeros(stat_send.shape, F32)
    for g in range(HEADS):
        stat_send[g, 0:2, :] = lse_t[2 * g : 2 * g + 2, :]
        stat_send[g, 2:4, :] = delta_t[2 * g : 2 * g + 2, :]
    own_stat = pltpu.make_async_copy(stat_send.at[head], ST.at[0, :, mine], s_loc.at[6])
    own_stat.start()
    for r in range(1, 8):
        exchange(4, r).start()

    def clear(i, _):
        for s in range(4):
            DQ[s, pl.ds(pl.multiple_of(i * 32, 32), 32), :] = jnp.zeros((32, ROWS), F32)
            for j in range(2):
                DKV[s, j, pl.ds(pl.multiple_of(i * 128, 128), 128), :] = jnp.zeros((128, HEAD), F32)
        return 0

    lax.fori_loop(0, 8, clear, 0)

    first = pl.multiple_of(x_lo * HALF, HALF)
    second = pl.multiple_of(HALF - x_lo * HALF, HALF)
    starts = (first, second)

    def send_q(slot, part):
        if part == 2:
            src, dst = ST.at[0], ST.at[slot]
        else:
            rows = pl.ds(starts[part], HALF)
            src, dst = QD.at[0, :, rows], QD.at[slot, :, rows]
        return remote(src, dst, s_q.at[slot, part], r_q.at[slot, part], q_dev[slot])

    def send_k(slot, part):
        rows = pl.ds(starts[part], HALF)
        src = KV.at[2 if slot == 3 else 0, :, rows]
        device = far_dev if slot == 2 else core_dev
        return remote(src, KV.at[slot, :, rows], s_k.at[slot, part], r_k.at[slot, part], device)

    def add_block(qs, q_lo, ks, k_lo, mask):
        q_rows, k_rows = pl.ds(q_lo, HALF), pl.ds(k_lo, HALF)
        dq, dk, dv = block(
            QD[qs, 0, q_rows, :],
            QD[qs, 1, q_rows, :],
            ST[qs, :, q_rows],
            KV[ks, 0, k_rows, :],
            KV[ks, 1, k_rows, :],
            mask,
        )
        for e, t, part in dq:
            DQ[qs, e * HEAD : (e + 1) * HEAD, pl.ds(pl.multiple_of(q_lo + t * TILE, TILE), TILE)] += part
        DKV[ks, 0, k_rows, :] += dk
        DKV[ks, 1, k_rows, :] += dv

    for copy in local[2:]:
        copy.wait()
    own_stat.wait()
    for r in (1, 2, 3):
        for i in range(5):
            exchange(i, r).wait_recv()
    for copy in (send_k(2, 0), send_k(1, 0), send_q(1, 0), send_q(2, 0)):
        copy.start()
    for r in (4, 5, 6, 7):
        for i in range(5):
            exchange(i, r).wait_recv()
    for copy in (send_k(2, 1), send_k(1, 1), send_q(1, 1), send_q(2, 1)):
        copy.start()
    for slot, part in ((1, 2), (2, 2), (3, 0), (3, 1), (3, 2)):
        send_q(slot, part).start()

    def own_diagonal(i, _):
        at = pl.multiple_of(i * HALF, HALF)
        add_block(0, at, 0, at, True)
        return 0

    lax.fori_loop(0, 2, own_diagonal, 0)
    add_block(0, HALF, 0, 0, False)

    def return_dq(slot):
        return remote(dq_send.at[slot - 1], dq_recv.at[slot - 1], s_dq.at[slot], r_dq.at[slot], back_dev[slot])

    def return_core(slot):
        return remote(DKV.at[slot], core_recv.at[slot // 2], s_dk.at[slot], r_dk.at[slot], core_dev)

    def return_far():
        return remote(far_send, far_recv, s_dk.at[2], r_dk.at[2], far_dev)

    def pack_dq(slot):
        def step(i, _):
            rows = pl.ds(pl.multiple_of(i * 32, 32), 32)
            dq_send[slot - 1, rows, :] = DQ[slot, rows, :].astype(BF16)
            return 0

        lax.fori_loop(0, 8, step, 0)
        return_dq(slot).start()

    def pair(n, _):
        q_step, r = n // 4, n % 4
        later = (q_step + 3) // 4
        qs = q_step
        ks = r + later * (3 - 2 * r)

        for slot in (1, 2, 3):

            @pl.when(n == slot)
            def _():
                for part in range(2):
                    send_k(slot, part).wait_recv()
                if slot == 2:
                    for part in range(2):
                        send_k(3, part).start()

            @pl.when(n == 4 * slot)
            def _():
                for part in range(3):
                    send_q(slot, part).wait_recv()

        q_inner = (inner + (qs + 1) // 2 + 2 * ((qs % 2) * (1 - qs // 2))) % 4
        k_outer = ((x_hi + ks // 2) % 2) * 2 + (core + ks % 2) % 2
        sel = order[2 * (inner * 4 + k_outer)] < order[2 * (q_inner * 4 + outer)]
        add_block(qs, HALF, ks, 0, False)

        def pick(lo, hi):
            return jnp.where(sel, lo, hi)

        dq, dk, dv = block(
            pick(QD[qs, 0, 0:HALF, :], QD[qs, 0, HALF:ROWS, :]),
            pick(QD[qs, 1, 0:HALF, :], QD[qs, 1, HALF:ROWS, :]),
            pick(ST[qs, :, 0:HALF], ST[qs, :, HALF:ROWS]),
            pick(KV[ks, 0, 0:HALF, :], KV[ks, 0, HALF:ROWS, :]),
            pick(KV[ks, 1, 0:HALF, :], KV[ks, 1, HALF:ROWS, :]),
            False,
        )
        for e, t, part in dq:
            zero = jnp.zeros_like(part)
            rows = slice(e * HEAD, (e + 1) * HEAD)
            DQ[qs, rows, t * TILE : (t + 1) * TILE] += jnp.where(sel, part, zero)
            DQ[qs, rows, HALF + t * TILE : HALF + (t + 1) * TILE] += jnp.where(sel, zero, part)
        for j, part in enumerate((dk, dv)):
            zero = jnp.zeros_like(part)
            DKV[ks, j, 0:HALF, :] += jnp.where(sel, part, zero)
            DKV[ks, j, HALF:ROWS, :] += jnp.where(sel, zero, part)

        for slot in (1, 2, 3):

            @pl.when(n == 4 * slot + 3)
            def _():
                pack_dq(slot)

        for slot, at in ((3, 12), (1, 14)):

            @pl.when(n == at)
            def _():
                return_core(slot).start()

        @pl.when(n == 13)
        def _():
            return_core(3).wait_recv()

            def step(i, _):
                rows = pl.ds(pl.multiple_of(i * 128, 128), 128)
                for j in range(2):
                    far_send[j, rows, :] = (DKV[2, j, rows, :] + core_recv[1, j, rows, :]).astype(BF16)
                return 0

            lax.fori_loop(0, 8, step, 0)
            return_far().start()

        return 0

    lax.fori_loop(1, 16, pair, 0)

    def give(kind, r):
        p = peer(r)
        rows = wide(p, PART)
        if kind == 0:
            src, dst = dq_fin.at[rows], dq_out.at[0, :, wide(head, 256)]
        elif kind == 1:
            src, dst = dkv_fin.at[0, rows], dk_out.at[0, :, wide(head, 128)]
        else:
            src, dst = dkv_fin.at[1, rows], dv_out.at[0, :, wide(head, 128)]
        if r == 0:
            return pltpu.make_async_copy(src, dst, s_out.at[kind, 0])
        return remote(src, dst, s_out.at[kind, r], r_out.at[kind, r], (p, inner, outer))

    return_core(1).wait_recv()
    return_far().wait_recv()
    for r in (4, 5, 6, 7, 1, 2, 3, 0):
        rows = wide(peer(r), PART)
        for j, scale in ((0, SCALE), (1, 1.0)):
            total = DKV[0, j, rows, :] + core_recv[0, j, rows, :] + far_recv[j, rows, :].astype(F32)
            dkv_fin[j, rows, :] = (total * scale).astype(BF16)
        give(1, r).start()
        give(2, r).start()
    for slot in (1, 2, 3):
        return_dq(slot).wait_recv()
    for r in (4, 5, 6, 7, 1, 2, 3, 0):
        rows = wide(peer(r), PART)
        for e in range(2):
            feats = slice(e * HEAD, (e + 1) * HEAD)
            total = DQ[0, feats, rows]
            for slot in range(3):
                total = total + dq_recv[slot, feats, rows].astype(F32)
            dq_fin[rows, feats] = (total * SCALE).T.astype(BF16)
        give(0, r).start()

    for r in range(1, 8):
        for i in range(5):
            exchange(i, r).wait_send()
    for slot in (1, 2, 3):
        for part in range(3):
            send_q(slot, part).wait_send()
        for part in range(2):
            send_k(slot, part).wait_send()
        return_dq(slot).wait_send()
    for slot in (1, 3):
        return_core(slot).wait_send()
    return_far().wait_send()
    for kind in range(3):
        for r in range(8):
            give(kind, r).wait()


def per_device(queries, key_input, value_input, outputs, output_gradient, log_sum_exp, block_order):
    any_space = pl.BlockSpec(memory_space=pl.ANY)
    dma = pltpu.SemaphoreType.DMA
    return pl.pallas_call(
        kernel,
        out_shape=(
            jax.ShapeDtypeStruct((1, PART, 2048), BF16),
            jax.ShapeDtypeStruct((1, PART, 1024), BF16),
            jax.ShapeDtypeStruct((1, PART, 1024), BF16),
        ),
        in_specs=[pl.BlockSpec(memory_space=pltpu.SMEM)]
        + [any_space] * 5
        + [pl.BlockSpec(memory_space=pltpu.VMEM)],
        out_specs=(any_space,) * 3,
        scratch_shapes=[
            pltpu.VMEM((PART, 2048), BF16),
            pltpu.VMEM((PART, 2048), BF16),
            pltpu.VMEM((HEADS, 8, PART), F32),
            pltpu.VMEM((4, 2, ROWS, 256), BF16),
            pltpu.VMEM((4, 2, ROWS, HEAD), BF16),
            pltpu.VMEM((4, 8, ROWS), F32),
            pltpu.VMEM((4, 256, ROWS), F32),
            pltpu.VMEM((4, 2, ROWS, HEAD), F32),
            pltpu.VMEM((3, 256, ROWS), BF16),
            pltpu.VMEM((3, 256, ROWS), BF16),
            pltpu.VMEM((2, 2, ROWS, HEAD), F32),
            pltpu.VMEM((2, ROWS, HEAD), BF16),
            pltpu.VMEM((2, ROWS, HEAD), BF16),
            pltpu.VMEM((ROWS, 256), BF16),
            pltpu.VMEM((2, ROWS, HEAD), BF16),
            dma((8,)),
            dma((5, 8)),
            dma((5, 8)),
            dma((4, 3)),
            dma((4, 3)),
            dma((4, 2)),
            dma((4, 2)),
            dma((4,)),
            dma((4,)),
            dma((4,)),
            dma((4,)),
            dma((3, 8)),
            dma((3, 8)),
        ],
        compiler_params=pltpu.CompilerParams(
            collective_id=0, has_side_effects=True, vmem_limit_bytes=56 * 1024 * 1024
        ),
        name="attention_backward",
    )(block_order, queries, key_input, value_input, outputs, output_gradient, log_sum_exp)


def solution(mesh):
    split = P(("inner", "outer"), "head", None)
    return jax.shard_map(
        per_device, mesh=mesh, in_specs=(split,) * 6 + (P(),), out_specs=(split,) * 3, check_vma=False
    )
```

time: 861 us -> 139 us (0.16)
  waiting for transfers between devices: 322 us -> 0 us
  other arithmetic: 179 us -> 0 us
  Pallas kernels: 0 us -> 133 us
  loops' own time: 109 us -> 0 us
  local copies, waits for them, and re-layouts: 97.4 us -> 5.1 us
  matrix products: 87.7 us -> 0 us
  starting transfers between devices: 46.2 us -> 0 us
  blocking collectives: 11.2 us -> 0 us
    ppermute x64 -> x0, waiting for transfers between devices: 281 us -> none  [from_behind(): return lax.ppermute(block, axis, route)]
    add x144 -> x0, other arithmetic: 165 us -> none  [the longest x32 47.4 us: contribute(): key_halves[key_side] = key_halves[key_side] + found[1]]
    pallas_call x0 -> x1, Pallas kernels: none -> 133 us  [per_device(): pl.pallas_call(kernel, out_shape=(jax.ShapeDtypeStruct((1, PART, 2048), B...]
    another operation x65 -> x0, loops' own time: 109 us -> none  [the longest x1 107 us: per_device(): finished = lax.fori_loop(0, group_count, joined_turn, initial)]
    dot_general x165 -> x0, matrix products: 87.7 us -> none  [the longest x33 22.5 us: attend(): jnp.einsum('qhgd,khd->hgqk', query_groups, key_row_block, preferred_eleme...]
    while x224 -> x0, local copies, waits for them, and re-layouts: 52.9 us -> none
    all_to_all x8 -> x0, waiting for transfers between devices: 40.8 us -> none  [the longest x1 7.4 us: per_device(): lax.all_to_all(grad_rows, 'head', split_axis=1, concat_axis=0, tiled=True)]
    all_to_all x8 -> x0, starting transfers between devices: 33.4 us -> none  [the longest x1 6.47 us: per_device(): lax.all_to_all(log_sum_exp.reshape(local_row_count, QUERY_HEADS), 'head',...]
  transfers between devices with their start and end apart: 72 -> 0, of which waited for: 40 -> 0; matrix products, arithmetic and copies ran while one was open for 12% -> 0% of each run, Pallas kernels for 0% -> 0%
where the time goes in v1:
time: 139 us; the launch traced here: 138 us
  Pallas kernels  133 us (96%)
  local copies, waits for them, and re-layouts  5.1 us (4%)
    pallas_call x1, Pallas kernels, per_device(): pl.pallas_call(kernel, out_shape=(jax.ShapeDtypeStruct((1, PART, 2048), B...  133 us
    unnamed x8, local copies, waits for them, and re-layouts  5.1 us

profile of v1, /device:TPU:0, one launch (start us, length us, event | category | flops | bytes accessed | tf_op | source)
XLA Modules:
  0.0 138.3 jit_solution(12621109377267725563)
XLA Ops:
  0.6 1.4 %copy.10.lse_in = f32[1,128,16]{2,1,0:T(8,128)} copy(f32[1,128,16]{1,2,0:T(8,128)} %param.12) | data formatting | bytes 16384 | tf_op args[5]
  2.1 132.6 %attention_backward.1 = (bf16[1,128,2048]{2,1,0:T(8,128)(2,1)}, bf16[1,128,1024]{2,1,0:T(8,128)(2,1)}, bf16[1,128,1024]{2,1,0:T(8,128)(2,1)}) custom-call(s32[32]{0:T(128)} %order.1, bf16[1,128,2048]{2,1,0:T(8,128)(2,1)} %q_in.1, bf16[1,128,1024]{2,1,0:T(8,128)(2,1)} %k_in.1, bf16[1,128,1024]{2,1,0:T(8,128)(2,1)} %v_in.1, bf16[1,128,2048]{2,1,0:T(8,128)(2,1)} %o_in.1, ...), custom_call_target="tpu_custom_call" | custom-call | tf_op jit(solution)/shard_map/attention_backward/pallas_call | solution.py:393
  134.6 0.0 copy-start.1
  134.6 1.9 %copy.14 = bf16[1,128,2048]{2,1,0:T(8,128)(2,1)} copy(bf16[1,128,2048]{2,1,0:T(8,128)(2,1)} %get-tuple-element.6) | data formatting | bytes 1048576
  136.6 0.0 copy-done.1
  136.6 0.0 copy-start
  136.6 0.7 copy.15
  137.3 0.3 copy-done
  137.6 0.7 copy.16
Async XLA Ops:
  134.6 1.9 %copy-start.1 = (bf16[1,128,1024]{2,1,0:T(8,128)(2,1)S(1)}, bf16[1,128,1024]{2,1,0:T(8,128)(2,1)}, u32[]{:S(2)}) copy-start(bf16[1,128,1024]{2,1,0:T(8,128)(2,1)} %get-tuple-element.7) | copy-start | bytes 786436
  136.6 1.0 copy-start

commit v2 on v1

v2 whole, which is shorter than its diff:
```python
import functools

import jax
import jax.numpy as jnp
from jax import lax
from jax.experimental import pallas as pl
from jax.experimental.pallas import tpu as pltpu
from jax.sharding import PartitionSpec as P

MESH = pl.DeviceIdType.MESH
F32, BF16 = jnp.float32, jnp.bfloat16
HEAD = 128
HEADS = 8
PART = 128
HALF = 512
ROWS = 1024
LOG2E = 1.4426950408889634
SCALE = HEAD**-0.5
TILE = 256
NT = (((1,), (1,)), ((), ()))


def remote(src, dst, send_sem, recv_sem, device):
    return pltpu.make_async_remote_copy(
        src_ref=src,
        dst_ref=dst,
        send_sem=send_sem,
        recv_sem=recv_sem,
        device_id=device,
        device_id_type=MESH,
    )


def dot(a, b):
    return jnp.dot(a, b, preferred_element_type=F32)


def dot_nt(a, b):
    return lax.dot_general(a, b, NT, preferred_element_type=F32)


def block(q, do, stats, k, v, mask, heads=(0, 1)):
    k_t = k.T
    dk = dv = None
    dq = []
    for e in heads:
        for t in range(HALF // TILE):
            cols = slice(t * TILE, (t + 1) * TILE)
            q_e = q[cols, e * HEAD : (e + 1) * HEAD]
            do_e = do[cols, e * HEAD : (e + 1) * HEAD]
            scores = dot_nt(k, q_e)
            probs = jnp.exp2(scores * (SCALE * LOG2E) - stats[e : e + 1, cols])
            if mask:
                key_id = lax.broadcasted_iota(jnp.int32, (HALF, TILE), 0)
                query_id = lax.broadcasted_iota(jnp.int32, (HALF, TILE), 1) + t * TILE
                probs = jnp.where(key_id <= query_id, probs, 0.0)
            prob_grad = dot_nt(v, do_e)
            score_grad = (probs * (prob_grad - stats[2 + e : 3 + e, cols])).astype(BF16)
            dv_e = dot(probs.astype(BF16), do_e)
            dk_e = dot(score_grad, q_e)
            dv = dv_e if dv is None else dv + dv_e
            dk = dk_e if dk is None else dk + dk_e
            dq.append((e, t, dot(k_t, score_grad)))
    return dq, dk, dv


def kernel(
    order,
    q_in,
    k_in,
    v_in,
    o_in,
    do_in,
    lse_in,
    dq_out,
    dk_out,
    dv_out,
    o_vm,
    do_vm,
    qd_send,
    kv_send,
    stat_send,
    QD,
    KV,
    ST,
    DQ,
    DKV,
    dq_send,
    dq_recv,
    core_recv,
    far_send,
    far_recv,
    dq_fin,
    dkv_fin,
    s_loc,
    s_a2a,
    r_a2a,
    s_q,
    r_q,
    s_k,
    r_k,
    s_dq,
    r_dq,
    s_dk,
    r_dk,
    s_out,
    r_out,
):
    head, inner, outer = lax.axis_index("head"), lax.axis_index("inner"), lax.axis_index("outer")
    x_lo, z = head // 4, head % 4
    x_hi, core = outer // 2, outer % 2

    def peer(r):
        return ((x_lo + r // 4) % 2) * 4 + (z + r % 4) % 4

    q_dev = {
        1: (head, (inner + 1) % 4, outer),
        2: (head, (inner + 3) % 4, outer),
        3: (head, (inner + 2) % 4, outer),
    }
    back_dev = {1: q_dev[2], 2: q_dev[1], 3: q_dev[3]}
    core_dev = (head, inner, x_hi * 2 + (core + 1) % 2)
    far_dev = (head, inner, ((x_hi + 1) % 2) * 2 + core)

    barrier = pltpu.get_barrier_semaphore()
    everyone = [(peer(r), inner, outer) for r in range(1, 8)] + [q_dev[1], q_dev[2], q_dev[3], core_dev, far_dev]
    for device in everyone:
        pl.semaphore_signal(barrier, inc=1, device_id=device, device_id_type=MESH)

    mine = pl.ds(pl.multiple_of(head * PART, PART), PART)

    def wide(p, n):
        return pl.ds(pl.multiple_of(p * n, n), n)

    def fetch(r, i):
        p = peer(r)
        src = (q_in, do_in, k_in, v_in)[i].at[0, :, wide(p, (256, 256, 128, 128)[i])]
        if r == 0:
            dst = (QD if i < 2 else KV).at[0, i % 2, mine]
        else:
            dst = (qd_send if i < 2 else kv_send).at[r, i % 2]
        return pltpu.make_async_copy(src, dst, s_loc.at[i, r])

    def exchange(i, r):
        p = peer(r)
        src, dst = [
            (qd_send.at[r], QD.at[0, :, mine]),
            (kv_send.at[r], KV.at[0, :, mine]),
            (stat_send.at[p], ST.at[0, :, mine]),
        ][i]
        return remote(src, dst, s_a2a.at[i, r], r_a2a.at[i, r], (p, inner, outer))

    turn = (4, 1, 5, 3, 7, 2, 6)
    for r in turn:
        for i in range(4):
            fetch(r, i).start()
    rows_in = [
        pltpu.make_async_copy(o_in.at[0], o_vm, s_loc.at[4, 0]),
        pltpu.make_async_copy(do_in.at[0], do_vm, s_loc.at[4, 1]),
    ]
    for copy in rows_in:
        copy.start()
    for i in range(4):
        fetch(0, i).start()
    pl.semaphore_wait(barrier, len(everyone))
    for r in turn:
        for i in range(4):
            fetch(r, i).wait()
        exchange(0, r).start()
        exchange(1, r).start()

    for copy in rows_in:
        copy.wait()
    lane = lax.broadcasted_iota(jnp.int32, (PART, 128), 1)
    delta = jnp.zeros((PART, 128), F32)
    for h in range(2 * HEADS):
        cols = slice(h * HEAD, (h + 1) * HEAD)
        total = jnp.sum(o_vm[:, cols].astype(F32) * do_vm[:, cols].astype(F32), axis=1, keepdims=True)
        delta = jnp.where(lane == h, total, delta)
    delta_t = delta.T
    lse_t = lse_in[0] * LOG2E
    stat_send[...] = jnp.zeros(stat_send.shape, F32)
    for g in range(HEADS):
        stat_send[g, 0:2, :] = lse_t[2 * g : 2 * g + 2, :]
        stat_send[g, 2:4, :] = delta_t[2 * g : 2 * g + 2, :]
    own_stat = pltpu.make_async_copy(stat_send.at[head], ST.at[0, :, mine], s_loc.at[4, 2])
    own_stat.start()
    for r in range(1, 8):
        exchange(2, r).start()

    def clear(i, _):
        for s in range(4):
            DQ[s, pl.ds(pl.multiple_of(i * 32, 32), 32), :] = jnp.zeros((32, ROWS), F32)
            for j in range(2):
                DKV[s, j, pl.ds(pl.multiple_of(i * 128, 128), 128), :] = jnp.zeros((128, HEAD), F32)
        return 0

    lax.fori_loop(0, 8, clear, 0)

    LO, HI = 0, 1

    def half(part):
        return pl.ds(part * HALF, HALF)

    def send_q(slot, part, what):
        rows = half(part)
        if what == "stats":
            src, dst = ST.at[0, :, rows], ST.at[slot, :, rows]
            return remote(src, dst, s_q.at[slot, part, 2], r_q.at[slot, part, 2], q_dev[slot])
        if slot < 3:
            src, dst = QD.at[0, :, rows], QD.at[slot, :, rows]
            return remote(src, dst, s_q.at[slot, part, 0], r_q.at[slot, part, 0], q_dev[slot])
        src, dst = QD.at[2 - what, what, rows], QD.at[3, what, rows]
        return remote(src, dst, s_q.at[3, part, what], r_q.at[3, part, what], q_dev[2 - what])

    def send_k(slot, part):
        rows = half(part)
        src = KV.at[2 if slot == 3 else 0, :, rows]
        device = far_dev if slot == 2 else core_dev
        return remote(src, KV.at[slot, :, rows], s_k.at[slot, part], r_k.at[slot, part], device)

    def add_block(qs, q_lo, ks, k_lo, mask, heads=(0, 1)):
        q_rows, k_rows = pl.ds(q_lo, HALF), pl.ds(k_lo, HALF)
        dq, dk, dv = block(
            QD[qs, 0, q_rows, :],
            QD[qs, 1, q_rows, :],
            ST[qs, :, q_rows],
            KV[ks, 0, k_rows, :],
            KV[ks, 1, k_rows, :],
            mask,
            heads,
        )
        for e, t, part in dq:
            DQ[qs, e * HEAD : (e + 1) * HEAD, pl.ds(pl.multiple_of(q_lo + t * TILE, TILE), TILE)] += part
        DKV[ks, 0, k_rows, :] += dk
        DKV[ks, 1, k_rows, :] += dv

    def add_either(qs, ks, heads=(0, 1)):
        q_inner = (inner + (qs + 1) // 2 + 2 * ((qs % 2) * (1 - qs // 2))) % 4
        k_outer = ((x_hi + ks // 2) % 2) * 2 + (core + ks % 2) % 2
        sel = order[2 * (inner * 4 + k_outer)] < order[2 * (q_inner * 4 + outer)]

        def pick(lo, hi):
            return jnp.where(sel, lo, hi)

        dq, dk, dv = block(
            pick(QD[qs, 0, 0:HALF, :], QD[qs, 0, HALF:ROWS, :]),
            pick(QD[qs, 1, 0:HALF, :], QD[qs, 1, HALF:ROWS, :]),
            pick(ST[qs, :, 0:HALF], ST[qs, :, HALF:ROWS]),
            pick(KV[ks, 0, 0:HALF, :], KV[ks, 0, HALF:ROWS, :]),
            pick(KV[ks, 1, 0:HALF, :], KV[ks, 1, HALF:ROWS, :]),
            False,
            heads,
        )
        for e, t, part in dq:
            zero = jnp.zeros_like(part)
            rows = slice(e * HEAD, (e + 1) * HEAD)
            DQ[qs, rows, t * TILE : (t + 1) * TILE] += jnp.where(sel, part, zero)
            DQ[qs, rows, HALF + t * TILE : HALF + (t + 1) * TILE] += jnp.where(sel, zero, part)
        for j, part in enumerate((dk, dv)):
            zero = jnp.zeros_like(part)
            DKV[ks, j, 0:HALF, :] += jnp.where(sel, part, zero)
            DKV[ks, j, HALF:ROWS, :] += jnp.where(sel, zero, part)

    def add_full(qs, ks, heads=(0, 1)):
        add_block(qs, HALF, ks, 0, False, heads)

    for i in range(4):
        fetch(0, i).wait()
    own_stat.wait()
    for part in (HI, LO):
        base = 4 * ((1 - x_lo) if part == HI else x_lo)
        for j in range(4):

            def arrived(r=base + j):
                for i in range(3):
                    exchange(i, r).wait_recv()

            if j == 0:
                pl.when(base > 0)(arrived)
            else:
                arrived()
        for slot in (2, 1):
            send_k(slot, part).start()
        for slot in (1, 2):
            send_q(slot, part, "stats").start()
            send_q(slot, part, 0).start()
    for part in (HI, LO):
        send_q(3, part, "stats").start()

    def own_diagonal(i, _):
        at = pl.multiple_of(i * HALF, HALF)
        add_block(0, at, 0, at, True)
        return 0

    lax.fori_loop(0, 2, own_diagonal, 0)
    add_block(0, HALF, 0, 0, False)

    def return_dq(slot, e):
        feats = pl.ds(e * HEAD, HEAD)
        src, dst = dq_send.at[slot - 1, feats], dq_recv.at[slot - 1, feats]
        return remote(src, dst, s_dq.at[slot, e], r_dq.at[slot, e], back_dev[slot])

    def return_core(slot):
        return remote(DKV.at[slot], core_recv.at[slot // 2], s_dk.at[slot], r_dk.at[slot], core_dev)

    def return_far():
        return remote(far_send, far_recv, s_dk.at[2], r_dk.at[2], far_dev)

    def pack_dq(slot, e):
        def step(i, _):
            rows = pl.ds(pl.multiple_of(e * HEAD + i * 32, 32), 32)
            dq_send[slot - 1, rows, :] = DQ[slot, rows, :].astype(BF16)
            return 0

        lax.fori_loop(0, HEAD // 32, step, 0)
        return_dq(slot, e).start()

    def own_queries(ks, _):
        for slot in (1, 2, 3):

            @pl.when(ks == slot)
            def _():
                for part in range(2):
                    send_k(slot, part).wait_recv()
                if slot == 2:
                    for part in range(2):
                        send_k(3, part).start()

        add_full(0, ks)
        add_either(0, ks)
        return 0

    lax.fori_loop(1, 4, own_queries, 0)

    def arrive_and_forward(slot, part):
        send_q(slot, part, "stats").wait_recv()
        send_q(slot, part, 0).wait_recv()
        send_q(3, part, 2 - slot).start()

    def near_full(m, _):
        for slot in (1, 2):

            @pl.when(m == slot - 1)
            def _():
                arrive_and_forward(slot, HI)

        add_full(1 + m // 4, 3 - m % 4)
        return 0

    lax.fori_loop(0, 8, near_full, 0)

    def near_either(m, _):
        for slot in (1, 2):

            @pl.when(m == slot - 1)
            def _():
                arrive_and_forward(slot, LO)

        add_either(1 + m // 4, 3 - m % 4)
        for slot in (1, 2):

            @pl.when(m == 4 * slot - 1)
            def _():
                for e in range(2):
                    pack_dq(slot, e)

        return 0

    lax.fori_loop(0, 8, near_either, 0)

    for part in (HI, LO):
        for what in ("stats", 0, 1):
            send_q(3, part, what).wait_recv()

    def far_queries(m, _):
        ks = 3 - m
        add_full(3, ks)
        add_either(3, ks)

        @pl.when(m == 0)
        def _():
            return_core(3).start()

        return 0

    lax.fori_loop(0, 2, far_queries, 0)
    return_core(3).wait_recv()

    def pack_far(i, _):
        rows = pl.ds(pl.multiple_of(i * 128, 128), 128)
        for j in range(2):
            far_send[j, rows, :] = (DKV[2, j, rows, :] + core_recv[1, j, rows, :]).astype(BF16)
        return 0

    lax.fori_loop(0, 8, pack_far, 0)
    return_far().start()

    for e in range(2):

        def last_queries(m, _):
            ks = 1 - m
            add_full(3, ks, (e,))
            add_either(3, ks, (e,))
            if e == 1:

                @pl.when(m == 0)
                def _():
                    return_core(1).start()

            return 0

        lax.fori_loop(0, 2, last_queries, 0)
        pack_dq(3, e)

    def give(kind, r):
        p = peer(r)
        rows = wide(p, PART)
        if kind < 2:
            src = dq_fin.at[kind, rows]
            dst = dq_out.at[0, :, pl.ds(pl.multiple_of(head * 256 + kind * HEAD, HEAD), HEAD)]
        else:
            src, dst = dkv_fin.at[kind - 2, rows], (dk_out, dv_out)[kind - 2].at[0, :, wide(head, HEAD)]
        if r == 0:
            return pltpu.make_async_copy(src, dst, s_out.at[kind, 0])
        return remote(src, dst, s_out.at[kind, r], r_out.at[kind, r], (p, inner, outer))

    def finish_dq(e):
        for slot in (1, 2, 3):
            return_dq(slot, e).wait_recv()
        feats = slice(e * HEAD, (e + 1) * HEAD)
        for r in (4, 5, 6, 7, 1, 2, 3, 0):
            rows = wide(peer(r), PART)
            total = DQ[0, feats, rows]
            for slot in range(3):
                total = total + dq_recv[slot, feats, rows].astype(F32)
            dq_fin[e, rows, :] = (total * SCALE).T.astype(BF16)
            give(e, r).start()

    finish_dq(0)
    return_core(1).wait_recv()
    return_far().wait_recv()
    for r in (4, 5, 6, 7, 1, 2, 3, 0):
        rows = wide(peer(r), PART)
        for j, scale in ((0, SCALE), (1, 1.0)):
            total = DKV[0, j, rows, :] + core_recv[0, j, rows, :] + far_recv[j, rows, :].astype(F32)
            dkv_fin[j, rows, :] = (total * scale).astype(BF16)
        give(2, r).start()
        give(3, r).start()
    finish_dq(1)

    for r in range(1, 8):
        for i in range(3):
            exchange(i, r).wait_send()
    for slot in (1, 2, 3):
        for part in range(2):
            for what in ("stats", 0, 1) if slot == 3 else ("stats", 0):
                send_q(slot, part, what).wait_send()
            send_k(slot, part).wait_send()
        for e in range(2):
            return_dq(slot, e).wait_send()
    for slot in (1, 3):
        return_core(slot).wait_send()
    return_far().wait_send()
    for kind in range(4):
        for r in range(8):
            give(kind, r).wait()


def per_device(queries, key_input, value_input, outputs, output_gradient, log_sum_exp, block_order):
    any_space = pl.BlockSpec(memory_space=pl.ANY)
    dma = pltpu.SemaphoreType.DMA
    return pl.pallas_call(
        kernel,
        out_shape=(
            jax.ShapeDtypeStruct((1, PART, 2048), BF16),
            jax.ShapeDtypeStruct((1, PART, 1024), BF16),
            jax.ShapeDtypeStruct((1, PART, 1024), BF16),
        ),
        in_specs=[pl.BlockSpec(memory_space=pltpu.SMEM)]
        + [any_space] * 5
        + [pl.BlockSpec(memory_space=pltpu.VMEM)],
        out_specs=(any_space,) * 3,
        scratch_shapes=[
            pltpu.VMEM((PART, 2048), BF16),
            pltpu.VMEM((PART, 2048), BF16),
            pltpu.VMEM((HEADS, 2, PART, 256), BF16),
            pltpu.VMEM((HEADS, 2, PART, HEAD), BF16),
            pltpu.VMEM((HEADS, 8, PART), F32),
            pltpu.VMEM((4, 2, ROWS, 256), BF16),
            pltpu.VMEM((4, 2, ROWS, HEAD), BF16),
            pltpu.VMEM((4, 8, ROWS), F32),
            pltpu.VMEM((4, 256, ROWS), F32),
            pltpu.VMEM((4, 2, ROWS, HEAD), F32),
            pltpu.VMEM((3, 256, ROWS), BF16),
            pltpu.VMEM((3, 256, ROWS), BF16),
            pltpu.VMEM((2, 2, ROWS, HEAD), F32),
            pltpu.VMEM((2, ROWS, HEAD), BF16),
            pltpu.VMEM((2, ROWS, HEAD), BF16),
            pltpu.VMEM((2, ROWS, HEAD), BF16),
            pltpu.VMEM((2, ROWS, HEAD), BF16),
            dma((5, 8)),
            dma((3, 8)),
            dma((3, 8)),
            dma((4, 2, 3)),
            dma((4, 2, 3)),
            dma((4, 2)),
            dma((4, 2)),
            dma((4, 2)),
            dma((4, 2)),
            dma((4,)),
            dma((4,)),
            dma((4, 8)),
            dma((4, 8)),
        ],
        compiler_params=pltpu.CompilerParams(
            collective_id=0, has_side_effects=True, vmem_limit_bytes=56 * 1024 * 1024
        ),
        name="attention_backward",
    )(block_order, queries, key_input, value_input, outputs, output_gradient, jnp.transpose(log_sum_exp, (0, 2, 1)))


def solution(mesh):
    split = P(("inner", "outer"), "head", None)
    return jax.shard_map(
        per_device, mesh=mesh, in_specs=(split,) * 6 + (P(),), out_specs=(split,) * 3, check_vma=False
    )
```

time: 139 us -> 110 us (0.79)
  Pallas kernels: 133 us -> 105 us
  local copies, waits for them, and re-layouts: 5.1 us -> 3.67 us
    pallas_call x1, Pallas kernels: 133 us -> 105 us  [per_device(): pl.pallas_call(kernel, out_shape=(jax.ShapeDtypeStruct((1, PART, 2048), B...]
    unnamed x8 -> x7, local copies, waits for them, and re-layouts: 5.1 us -> 3.67 us
where the time goes in v2:
time: 110 us; the launch traced here: 109 us
  Pallas kernels  105 us (95%)
  local copies, waits for them, and re-layouts  3.67 us (3%)
    pallas_call x1, Pallas kernels, per_device(): pl.pallas_call(kernel, out_shape=(jax.ShapeDtypeStruct((1, PART, 2048), B...  105 us
    unnamed x7, local copies, waits for them, and re-layouts  3.67 us

profile of v2, /device:TPU:0, one launch (start us, length us, event | category | flops | bytes accessed | tf_op | source)
XLA Modules:
  0.0 108.9 jit_solution(10292174219359077080)
XLA Ops:
  0.6 104.5 %attention_backward.1 = (bf16[1,128,2048]{2,1,0:T(8,128)(2,1)}, bf16[1,128,1024]{2,1,0:T(8,128)(2,1)}, bf16[1,128,1024]{2,1,0:T(8,128)(2,1)}) custom-call(s32[32]{0:T(128)} %order.1, bf16[1,128,2048]{2,1,0:T(8,128)(2,1)} %q_in.1, bf16[1,128,1024]{2,1,0:T(8,128)(2,1)} %k_in.1, bf16[1,128,1024]{2,1,0:T(8,128)(2,1)} %v_in.1, bf16[1,128,2048]{2,1,0:T(8,128)(2,1)} %o_in.1, ...), custom_call_target="tpu_custom_call" | custom-call | tf_op jit(solution)/shard_map/attention_backward/pallas_call | solution.py:473
  105.2 0.0 copy-start.1
  105.2 1.9 %copy.13 = bf16[1,128,2048]{2,1,0:T(8,128)(2,1)} copy(bf16[1,128,2048]{2,1,0:T(8,128)(2,1)} %get-tuple-element.6) | data formatting | bytes 1048576
  107.1 0.0 copy-done.1
  107.1 0.0 copy-start
  107.1 0.7 copy.14
  107.8 0.3 copy-done
  108.2 0.7 copy.15
Async XLA Ops:
  105.2 1.9 %copy-start.1 = (bf16[1,128,1024]{2,1,0:T(8,128)(2,1)S(1)}, bf16[1,128,1024]{2,1,0:T(8,128)(2,1)}, u32[]{:S(2)}) copy-start(bf16[1,128,1024]{2,1,0:T(8,128)(2,1)} %get-tuple-element.7) | copy-start | bytes 786436
  107.1 1.0 copy-start

commit v3 on v2

v3 whole, which is shorter than its diff:
```python
import functools

import jax
import jax.numpy as jnp
from jax import lax
from jax.experimental import pallas as pl
from jax.experimental.pallas import tpu as pltpu
from jax.sharding import PartitionSpec as P

MESH = pl.DeviceIdType.MESH
F32, BF16 = jnp.float32, jnp.bfloat16
HEAD = 128
HEADS = 8
PART = 128
HALF = 512
ROWS = 1024
LOG2E = 1.4426950408889634
SCALE = HEAD**-0.5
TILE = 256
NT = (((1,), (1,)), ((), ()))


def remote(src, dst, send_sem, recv_sem, device):
    return pltpu.make_async_remote_copy(
        src_ref=src,
        dst_ref=dst,
        send_sem=send_sem,
        recv_sem=recv_sem,
        device_id=device,
        device_id_type=MESH,
    )


def dot(a, b):
    return jnp.dot(a, b, preferred_element_type=F32)


def dot_nt(a, b):
    return lax.dot_general(a, b, NT, preferred_element_type=F32)


def block(q, do, stats, k, v, mask, heads):
    tiles = [(e, t) for e in heads for t in range(HALF // TILE)]

    def products(e, t):
        rows, feats = slice(t * TILE, (t + 1) * TILE), slice(e * HEAD, (e + 1) * HEAD)
        return dot_nt(k, q[rows, feats]), dot_nt(v, do[rows, feats])

    probs_low, score_grads = [], []
    ahead = products(*tiles[0])
    for n, (e, t) in enumerate(tiles):
        scores, prob_grad = ahead
        if n + 1 < len(tiles):
            ahead = products(*tiles[n + 1])
        cols = slice(t * TILE, (t + 1) * TILE)
        probs = jnp.exp2(scores * (SCALE * LOG2E) - stats[e : e + 1, cols])
        if mask:
            key_id = lax.broadcasted_iota(jnp.int32, (HALF, TILE), 0)
            query_id = lax.broadcasted_iota(jnp.int32, (HALF, TILE), 1) + t * TILE
            probs = jnp.where(key_id <= query_id, probs, 0.0)
        score_grads.append((probs * (prob_grad - stats[2 + e : 3 + e, cols])).astype(BF16))
        probs_low.append(probs.astype(BF16))
    probs_low = jnp.concatenate(probs_low, axis=1)
    score_grads = jnp.concatenate(score_grads, axis=1)

    def stacked(x):
        return jnp.concatenate([x[:, e * HEAD : (e + 1) * HEAD] for e in heads], axis=0)

    dv = dot(probs_low, stacked(do))
    dk = dot(score_grads, stacked(q))
    dq = dot(k.T, score_grads)
    return [(e, dq[:, i * HALF : (i + 1) * HALF]) for i, e in enumerate(heads)], dk, dv


def kernel(
    order,
    q_in,
    k_in,
    v_in,
    o_in,
    do_in,
    lse_in,
    dq_out,
    dk_out,
    dv_out,
    o_vm,
    do_vm,
    qd_send,
    kv_send,
    stat_send,
    far_stage,
    QD,
    KV,
    ST,
    DQ,
    DKV,
    dkv_send,
    dkv_recv,
    core_recv,
    dq_fin,
    dq_part,
    dkv_fin,
    s_loc,
    s_a2a,
    r_a2a,
    s_q,
    r_q,
    s_k,
    r_k,
    s_dq,
    r_dq,
    s_dk,
    r_dk,
    s_far,
    r_far,
    s_stage,
    r_stage,
    s_dqo,
    r_dqo,
    s_out,
    r_out,
):
    head, inner, outer = lax.axis_index("head"), lax.axis_index("inner"), lax.axis_index("outer")
    x_lo, z = head // 4, head % 4
    x_hi, core = outer // 2, outer % 2

    def peer(r):
        return ((x_lo + r // 4) % 2) * 4 + (z + r % 4) % 4

    k_dev = {
        1: (head, (inner + 1) % 4, outer),
        2: (head, (inner + 3) % 4, outer),
        3: (head, (inner + 2) % 4, outer),
    }
    back_dev = {1: k_dev[2], 2: k_dev[1], 3: k_dev[3]}
    core_dev = (head, inner, x_hi * 2 + (core + 1) % 2)
    far_outer = ((x_hi + 1) % 2) * 2 + core

    barrier = pltpu.get_barrier_semaphore()
    everyone = [(peer(r), inner, outer) for r in range(1, 8)] + [(peer(r), inner, far_outer) for r in range(8)]
    everyone += [k_dev[1], k_dev[2], k_dev[3], core_dev]
    for device in everyone:
        pl.semaphore_signal(barrier, inc=1, device_id=device, device_id_type=MESH)

    mine = pl.ds(pl.multiple_of(head * PART, PART), PART)

    def wide(p, n):
        return pl.ds(pl.multiple_of(p * n, n), n)

    def fetch(r, i):
        p = peer(r)
        src = (q_in, do_in, k_in, v_in)[i].at[0, :, wide(p, (256, 256, 128, 128)[i])]
        if r == 0:
            dst = (QD if i < 2 else KV).at[0, i % 2, mine]
        else:
            dst = (qd_send if i < 2 else kv_send).at[r, i % 2]
        return pltpu.make_async_copy(src, dst, s_loc.at[i, r])

    def exchange(i, r):
        p = peer(r)
        src, dst = [
            (qd_send.at[r], QD.at[0, :, mine]),
            (kv_send.at[r], KV.at[0, :, mine]),
            (stat_send.at[p], ST.at[0, :, mine]),
        ][i]
        return remote(src, dst, s_a2a.at[i, r], r_a2a.at[i, r], (p, inner, outer))

    def to_far(kind, r):
        p = peer(r)
        if kind == 0:
            src, dst = QD.at[0, :, mine] if r == 0 else qd_send.at[r], QD.at[2, :, mine]
        else:
            src, dst = stat_send.at[p], ST.at[2, :, mine]
        return remote(src, dst, s_far.at[kind, r], r_far.at[kind, r], (p, inner, far_outer))

    def to_stage():
        src = qd_send.at[pl.ds(5, 3)]
        return remote(src, far_stage, s_far.at[0, 5], r_far.at[0, 5], (peer(4), inner, far_outer))

    def from_stage(b):
        rows = wide(peer(4), PART)
        device = (x_lo * 4 + (z + b) % 4, inner, outer)
        return remote(far_stage.at[b - 1], QD.at[2, :, rows], s_stage.at[b], r_stage.at[b], device)

    turn = (4, 1, 5, 3, 7, 2, 6)
    for pick in ((2, 3), (0, 1)):
        for r in turn:
            for i in pick:
                fetch(r, i).start()
    for i in range(4):
        fetch(0, i).start()
    rows_in = [
        pltpu.make_async_copy(o_in.at[0], o_vm, s_loc.at[4, 0]),
        pltpu.make_async_copy(do_in.at[0], do_vm, s_loc.at[4, 1]),
    ]
    for copy in rows_in:
        copy.start()
    pl.semaphore_wait(barrier, len(everyone))
    for r in turn:
        for i in (2, 3):
            fetch(r, i).wait()
        exchange(1, r).start()

    for r in (4, 5, 6, 7):
        for i in (0, 1):
            fetch(r, i).wait()
    to_far(0, 4).start()
    to_stage().start()

    for copy in rows_in:
        copy.wait()
    lane = lax.broadcasted_iota(jnp.int32, (PART, 128), 1)
    delta = jnp.zeros((PART, 128), F32)
    for h in range(2 * HEADS):
        cols = slice(h * HEAD, (h + 1) * HEAD)
        total = jnp.sum(o_vm[:, cols].astype(F32) * do_vm[:, cols].astype(F32), axis=1, keepdims=True)
        delta = jnp.where(lane == h, total, delta)
    delta_t = delta.T
    lse_t = lse_in[0] * LOG2E
    stat_send[...] = jnp.zeros(stat_send.shape, F32)
    for g in range(HEADS):
        stat_send[g, 0:2, :] = lse_t[2 * g : 2 * g + 2, :]
        stat_send[g, 2:4, :] = delta_t[2 * g : 2 * g + 2, :]
    own_stat = pltpu.make_async_copy(stat_send.at[head], ST.at[0, :, mine], s_loc.at[4, 2])
    own_stat.start()
    for r in range(1, 8):
        exchange(2, r).start()
    for r in range(8):
        to_far(1, r).start()

    def clear(i, _):
        for s in range(4):
            DQ[s, pl.ds(pl.multiple_of(i * 32, 32), 32), :] = jnp.zeros((32, ROWS), F32)
            for j in range(2):
                DKV[s, j, pl.ds(pl.multiple_of(i * 128, 128), 128), :] = jnp.zeros((128, HEAD), F32)
        return 0

    lax.fori_loop(0, 8, clear, 0)

    LO, HI = 0, 1

    def half(part):
        return pl.ds(part * HALF, HALF)

    def send_q(slot, part, what):
        rows = half(part)
        array = ST if what else QD
        src = array.at[2 if slot == 3 else 0, :, rows]
        return remote(src, array.at[slot, :, rows], s_q.at[slot, part, what], r_q.at[slot, part, what], core_dev)

    def send_k(slot, part, what):
        rows = half(part)
        if slot < 3:
            src, dst = KV.at[0, :, rows], KV.at[slot, :, rows]
            return remote(src, dst, s_k.at[slot, part, 0], r_k.at[slot, part, 0], k_dev[slot])
        src, dst = KV.at[2 - what, what, rows], KV.at[3, what, rows]
        return remote(src, dst, s_k.at[3, part, what], r_k.at[3, part, what], k_dev[2 - what])

    def add_block(qs, q_lo, ks, k_lo, mask, heads=(0, 1)):
        q_rows, k_rows = pl.ds(q_lo, HALF), pl.ds(k_lo, HALF)
        dq, dk, dv = block(
            QD[qs, 0, q_rows, :],
            QD[qs, 1, q_rows, :],
            ST[qs, :, q_rows],
            KV[ks, 0, k_rows, :],
            KV[ks, 1, k_rows, :],
            mask,
            heads,
        )
        for e, part in dq:
            DQ[qs, e * HEAD : (e + 1) * HEAD, q_rows] += part
        DKV[ks, 0, k_rows, :] += dk
        DKV[ks, 1, k_rows, :] += dv

    def add_either(qs, ks, heads=(0, 1)):
        q_outer = ((x_hi + qs // 2) % 2) * 2 + (core + qs % 2) % 2
        k_inner = (inner + (ks + 1) // 2 + 2 * ((ks % 2) * (1 - ks // 2))) % 4
        sel = order[2 * (k_inner * 4 + outer)] < order[2 * (inner * 4 + q_outer)]

        def pick(lo, hi):
            return jnp.where(sel, lo, hi)

        dq, dk, dv = block(
            pick(QD[qs, 0, 0:HALF, :], QD[qs, 0, HALF:ROWS, :]),
            pick(QD[qs, 1, 0:HALF, :], QD[qs, 1, HALF:ROWS, :]),
            pick(ST[qs, :, 0:HALF], ST[qs, :, HALF:ROWS]),
            pick(KV[ks, 0, 0:HALF, :], KV[ks, 0, HALF:ROWS, :]),
            pick(KV[ks, 1, 0:HALF, :], KV[ks, 1, HALF:ROWS, :]),
            False,
            heads,
        )
        for e, part in dq:
            zero = jnp.zeros_like(part)
            rows = slice(e * HEAD, (e + 1) * HEAD)
            DQ[qs, rows, 0:HALF] += jnp.where(sel, part, zero)
            DQ[qs, rows, HALF:ROWS] += jnp.where(sel, zero, part)
        for j, part in enumerate((dk, dv)):
            zero = jnp.zeros_like(part)
            DKV[ks, j, 0:HALF, :] += jnp.where(sel, part, zero)
            DKV[ks, j, HALF:ROWS, :] += jnp.where(sel, zero, part)

    def add_full(qs, ks, heads=(0, 1)):
        add_block(qs, HALF, ks, 0, False, heads)

    def wait_half(part, kinds):
        base = 4 * ((1 - x_lo) if part == HI else x_lo)
        for j in range(4):

            def arrived(r=base + j):
                for kind in kinds:
                    exchange(kind, r).wait_recv()

            if j == 0:
                pl.when(base > 0)(arrived)
            else:
                arrived()

    def near_keys(part):
        for slot in (1, 2):
            send_k(slot, part, 0).wait_recv()
            send_k(3, part, 2 - slot).start()

    for r in turn:
        for i in (0, 1):
            if r < 4:
                fetch(r, i).wait()
        exchange(1, r).wait_send()
        exchange(0, r).start()
    for i in range(4):
        fetch(0, i).wait()
    for part in (LO, HI):
        wait_half(part, (1,))
        for slot in (1, 2):
            send_k(slot, part, 0).start()
    near_keys(LO)
    own_stat.wait()
    for part in (HI, LO):
        wait_half(part, (2, 0))
        for what in (1, 0):
            send_q(1, part, what).start()
    to_stage().wait_recv()
    for b in (1, 3, 2):
        from_stage(b).start()
        to_far(0, b).start()
    to_far(0, 0).start()

    def arrived_queries(slot, part):
        for what in (1, 0):
            send_q(slot, part, what).wait_recv()

    def far_to_core(part):
        crossed = (1 - x_lo) if part == HI else x_lo

        @pl.when(crossed == 1)
        def _():
            to_far_in(0, 4).wait_recv()
            for b in (1, 2, 3):
                from_stage(b).wait_recv()

        @pl.when(crossed == 0)
        def _():
            for r in range(4):
                to_far_in(0, r).wait_recv()

        for j in range(4):
            to_far_in(1, 4 * crossed + j).wait_recv()
        for what in (1, 0):
            send_q(3, part, what).start()

    def to_far_in(kind, r):
        dst = (ST if kind else QD).at[2, :, mine]
        return remote(dst, dst, s_far.at[kind, r], r_far.at[kind, r], (head, inner, far_outer))

    def return_core(slot, e):
        feats = pl.ds(e * HEAD, HEAD)
        src, dst = DQ.at[slot, feats], core_recv.at[slot // 2, feats]
        return remote(src, dst, s_dq.at[slot, e], r_dq.at[slot, e], core_dev)

    def return_dkv(slot, j):
        src, dst = dkv_send.at[slot - 1, j], dkv_recv.at[slot - 1, j]
        return remote(src, dst, s_dk.at[slot, j], r_dk.at[slot, j], back_dev[slot])

    def own_diagonal(i, _):
        at = pl.multiple_of(i * HALF, HALF)
        add_block(0, at, 0, at, True)
        return 0

    lax.fori_loop(0, 2, own_diagonal, 0)
    add_full(0, 0)
    near_keys(HI)
    for part in (HI, LO):
        arrived_queries(1, part)
    add_full(1, 0)
    add_either(1, 0)

    def near_queries(n, _):
        qs, ks = n % 2, 1 + n // 2

        for at, part in ((4, HI), (5, LO)):

            @pl.when(n == at)
            def _():
                far_to_core(part)

        @pl.when(n == 4)
        def _():
            for part in (LO, HI):
                for what in range(2):
                    send_k(3, part, what).wait_recv()

        add_full(qs, ks)
        add_either(qs, ks)
        return 0

    lax.fori_loop(0, 6, near_queries, 0)

    for e in range(2):
        return_core(1, e).start()
    back = (4, 1, 5, 3, 7, 2, 6, 0)

    def transpose_dq(far, e, r):
        rows, feats = wide(peer(r), PART), slice(e * HEAD, (e + 1) * HEAD)
        total = DQ[2 * far, feats, rows] + core_recv[far, feats, rows]
        dq_fin[far, e, rows, :] = (total * SCALE).T.astype(BF16)

    def give_dq(far, e, r):
        p = peer(r)
        src, dst = dq_fin.at[far, e, wide(p, PART)], dq_part.at[far, head, e]
        if not far and r == 0:
            return pltpu.make_async_copy(src, dst, s_dqo.at[0, e, 0])
        device = (p, inner, far_outer if far else outer)
        return remote(src, dst, s_dqo.at[far, e, r], r_dqo.at[far, e, r], device)

    def send_rows(far, e):
        return_core(3 if far else 1, e).wait_recv()
        for r in back:
            transpose_dq(far, e, r)
            give_dq(far, e, r).start()

    def far_queries(m, _):
        i = m // 2
        qs, ks = 2 + m % 2, i + 3 * ((3 - i) // 3)

        @pl.when(m == 1)
        def _():
            for part in (HI, LO):
                arrived_queries(3, part)

        add_full(qs, ks)
        add_either(qs, ks)
        @pl.when(m == 1)
        def _():
            for e in range(2):
                send_rows(0, e)

        for at, slot in ((1, 3), (3, 1), (5, 2)):

            @pl.when(m == at)
            def _():
                for j in range(2):

                    def step(i, _):
                        rows = pl.ds(pl.multiple_of(i * 128, 128), 128)
                        dkv_send[slot - 1, j, rows, :] = DKV[slot, j, rows, :].astype(BF16)
                        return 0

                    lax.fori_loop(0, 8, step, 0)
                    return_dkv(slot, j).start()

        return 0

    lax.fori_loop(0, 6, far_queries, 0)

    for e in range(2):
        add_full(3, 0, (e,))
        add_either(3, 0, (e,))
        return_core(3, e).start()
        if e == 1:
            send_rows(1, 0)
        add_full(2, 0, (e,))
        add_either(2, 0, (e,))
    send_rows(1, 1)

    def give(kind, r):
        p = peer(r)
        src, dst = dkv_fin.at[kind, wide(p, PART)], (dk_out, dv_out)[kind].at[0, :, wide(head, HEAD)]
        if r == 0:
            return pltpu.make_async_copy(src, dst, s_out.at[kind, 0])
        return remote(src, dst, s_out.at[kind, r], r_out.at[kind, r], (p, inner, outer))

    for j, scale in ((0, SCALE), (1, 1.0)):
        for slot in (3, 1, 2):
            return_dkv(slot, j).wait_recv()
        for r in back:
            rows = wide(peer(r), PART)
            total = DKV[0, j, rows, :]
            for slot in range(3):
                total = total + dkv_recv[slot, j, rows, :].astype(F32)
            dkv_fin[j, rows, :] = (total * scale).astype(BF16)
            give(j, r).start()

    for e in range(2):
        for far in range(2):
            for r in range(8):
                give_dq(far, e, r).wait()
        for g in range(HEADS):
            total = dq_part[0, g, e].astype(F32) + dq_part[1, g, e].astype(F32)
            dq_out[0, :, g * 256 + e * HEAD : g * 256 + (e + 1) * HEAD] = total.astype(BF16)

    for r in range(1, 8):
        for i in (0, 2):
            exchange(i, r).wait_send()
    for r in range(8):
        to_far(1, r).wait_send()
    for r in range(5):
        to_far(0, r).wait_send()
    to_stage().wait_send()
    for b in (1, 2, 3):
        from_stage(b).wait_send()
    for slot in (1, 2, 3):
        for part in range(2):
            for what in range(2):
                if slot != 2:
                    send_q(slot, part, what).wait_send()
            for what in range(2 if slot == 3 else 1):
                send_k(slot, part, what).wait_send()
        for j in range(2):
            return_dkv(slot, j).wait_send()
    for slot in (1, 3):
        for e in range(2):
            return_core(slot, e).wait_send()
    for kind in range(2):
        for r in range(8):
            give(kind, r).wait()


def copy_kernel(dq, dk, dv, dq_out, dk_out, dv_out):
    for src, dst in ((dq, dq_out), (dk, dk_out), (dv, dv_out)):
        dst[...] = src[...]


def per_device(queries, key_input, value_input, outputs, output_gradient, log_sum_exp, block_order):
    any_space = pl.BlockSpec(memory_space=pl.ANY)
    dma = pltpu.SemaphoreType.DMA
    grads = pl.pallas_call(
        kernel,
        out_shape=(
            jax.ShapeDtypeStruct((1, PART, 2048), BF16),
            jax.ShapeDtypeStruct((1, PART, 1024), BF16),
            jax.ShapeDtypeStruct((1, PART, 1024), BF16),
        ),
        in_specs=[pl.BlockSpec(memory_space=pltpu.SMEM)]
        + [any_space] * 5
        + [pl.BlockSpec(memory_space=pltpu.VMEM)],
        out_specs=(pl.BlockSpec(memory_space=pltpu.VMEM), any_space, any_space),
        scratch_shapes=[
            pltpu.VMEM((PART, 2048), BF16),
            pltpu.VMEM((PART, 2048), BF16),
            pltpu.VMEM((HEADS, 2, PART, 256), BF16),
            pltpu.VMEM((HEADS, 2, PART, HEAD), BF16),
            pltpu.VMEM((HEADS, 8, PART), F32),
            pltpu.VMEM((3, 2, PART, 256), BF16),
            pltpu.VMEM((4, 2, ROWS, 256), BF16),
            pltpu.VMEM((4, 2, ROWS, HEAD), BF16),
            pltpu.VMEM((4, 8, ROWS), F32),
            pltpu.VMEM((4, 256, ROWS), F32),
            pltpu.VMEM((4, 2, ROWS, HEAD), F32),
            pltpu.VMEM((3, 2, ROWS, HEAD), BF16),
            pltpu.VMEM((3, 2, ROWS, HEAD), BF16),
            pltpu.VMEM((2, 256, ROWS), F32),
            pltpu.VMEM((2, 2, ROWS, HEAD), BF16),
            pltpu.VMEM((2, HEADS, 2, PART, HEAD), BF16),
            pltpu.VMEM((2, ROWS, HEAD), BF16),
            dma((5, 8)),
            dma((3, 8)),
            dma((3, 8)),
            dma((4, 2, 2)),
            dma((4, 2, 2)),
            dma((4, 2, 2)),
            dma((4, 2, 2)),
            dma((4, 2)),
            dma((4, 2)),
            dma((4, 2)),
            dma((4, 2)),
            dma((2, 8)),
            dma((2, 8)),
            dma((4,)),
            dma((4,)),
            dma((2, 2, 8)),
            dma((2, 2, 8)),
            dma((2, 8)),
            dma((2, 8)),
        ],
        compiler_params=pltpu.CompilerParams(
            collective_id=0, has_side_effects=True, vmem_limit_bytes=56 * 1024 * 1024
        ),
        name="attention_backward",
    )(block_order, queries, key_input, value_input, outputs, output_gradient, jnp.transpose(log_sum_exp, (0, 2, 1)))
    whole = pl.BlockSpec(memory_space=pltpu.VMEM)
    return pl.pallas_call(
        copy_kernel,
        out_shape=tuple(jax.ShapeDtypeStruct(g.shape, g.dtype) for g in grads),
        in_specs=[whole] * 3,
        out_specs=(whole,) * 3,
        name="copy_out",
    )(*grads)


def solution(mesh):
    split = P(("inner", "outer"), "head", None)
    return jax.shard_map(
        per_device, mesh=mesh, in_specs=(split,) * 6 + (P(),), out_specs=(split,) * 3, check_vma=False
    )
```

time: 110 us -> 96.4 us (0.88)
  Pallas kernels: 105 us -> 94.8 us
  local copies, waits for them, and re-layouts: 3.67 us -> 0 us
    pallas_call x1, Pallas kernels: 105 us -> 92.7 us  [per_device(): pl.pallas_call(kernel, out_shape=(jax.ShapeDtypeStruct((1, PART, 2048), B...]
    unnamed x7 -> x0, local copies, waits for them, and re-layouts: 3.67 us -> none
    pallas_call x0 -> x1, Pallas kernels: none -> 2.17 us  [per_device(): pl.pallas_call(copy_kernel, out_shape=tuple((jax.ShapeDtypeStruct(g.shape...]
where the time goes in v3:
time: 96.4 us; the launch traced here: 95.5 us
  Pallas kernels  94.8 us (98%)
    pallas_call x1, Pallas kernels, per_device(): pl.pallas_call(kernel, out_shape=(jax.ShapeDtypeStruct((1, PART, 2048), B...  92.7 us
    pallas_call x1, Pallas kernels, per_device(): pl.pallas_call(copy_kernel, out_shape=tuple((jax.ShapeDtypeStruct(g.shape...  2.17 us

profile of v3, /device:TPU:0, one launch (start us, length us, event | category | flops | bytes accessed | tf_op | source)
XLA Modules:
  0.0 95.5 jit_solution(11382282316122865761)
XLA Ops:
  0.6 92.7 %attention_backward.1 = (bf16[1,128,2048]{2,1,0:T(8,128)(2,1)}, bf16[1,128,1024]{2,1,0:T(8,128)(2,1)}, bf16[1,128,1024]{2,1,0:T(8,128)(2,1)}) custom-call(s32[32]{0:T(128)} %order.1, bf16[1,128,2048]{2,1,0:T(8,128)(2,1)} %q_in.1, bf16[1,128,1024]{2,1,0:T(8,128)(2,1)} %k_in.1, bf16[1,128,1024]{2,1,0:T(8,128)(2,1)} %v_in.1, bf16[1,128,2048]{2,1,0:T(8,128)(2,1)} %o_in.1, ...), custom_call_target="tpu_custom_call" | custom-call | tf_op jit(solution)/shard_map/attention_backward/pallas_call | solution.py:545
  93.3 2.2 %copy_out.1 = (bf16[1,128,2048]{2,1,0:T(8,128)(2,1)}, bf16[1,128,1024]{2,1,0:T(8,128)(2,1)}, bf16[1,128,1024]{2,1,0:T(8,128)(2,1)}) custom-call(bf16[1,128,2048]{2,1,0:T(8,128)(2,1)} %get-tuple-element.6.dq, bf16[1,128,1024]{2,1,0:T(8,128)(2,1)} %get-tuple-element.7.dk, bf16[1,128,1024]{2,1,0:T(8,128)(2,1)} %get-tuple-element.8.dv), custom_call_target="tpu_custom_call" | custom-call | tf_op jit(solution)/shard_map/copy_out/pallas_call | solution.py:600

commit v4 on v3

--- a/solution.py
+++ b/solution.py
@@ -40,7 +40,8 @@
 
 
 def block(q, do, stats, k, v, mask, heads):
-    tiles = [(e, t) for e in heads for t in range(HALF // TILE)]
+    queries, keys = q.shape[0], k.shape[0]
+    tiles = [(e, t) for e in heads for t in range(queries // TILE)]
 
     def products(e, t):
         rows, feats = slice(t * TILE, (t + 1) * TILE), slice(e * HEAD, (e + 1) * HEAD)
@@ -54,9 +55,9 @@
             ahead = products(*tiles[n + 1])
         cols = slice(t * TILE, (t + 1) * TILE)
         probs = jnp.exp2(scores * (SCALE * LOG2E) - stats[e : e + 1, cols])
-        if mask:
-            key_id = lax.broadcasted_iota(jnp.int32, (HALF, TILE), 0)
-            query_id = lax.broadcasted_iota(jnp.int32, (HALF, TILE), 1) + t * TILE
+        if mask and t * TILE < keys:
+            key_id = lax.broadcasted_iota(jnp.int32, (keys, TILE), 0)
+            query_id = lax.broadcasted_iota(jnp.int32, (keys, TILE), 1) + t * TILE
             probs = jnp.where(key_id <= query_id, probs, 0.0)
         score_grads.append((probs * (prob_grad - stats[2 + e : 3 + e, cols])).astype(BF16))
         probs_low.append(probs.astype(BF16))
@@ -69,7 +70,7 @@
     dv = dot(probs_low, stacked(do))
     dk = dot(score_grads, stacked(q))
     dq = dot(k.T, score_grads)
-    return [(e, dq[:, i * HALF : (i + 1) * HALF]) for i, e in enumerate(heads)], dk, dv
+    return [(e, dq[:, i * queries : (i + 1) * queries]) for i, e in enumerate(heads)], dk, dv
 
 
 def kernel(
@@ -235,12 +236,11 @@
                 DKV[s, j, pl.ds(pl.multiple_of(i * 128, 128), 128), :] = jnp.zeros((128, HEAD), F32)
         return 0
 
-    lax.fori_loop(0, 8, clear, 0)
 
     LO, HI = 0, 1
 
     def half(part):
-        return pl.ds(part * HALF, HALF)
+        return pl.ds(pl.multiple_of(part * HALF, HALF), HALF)
 
     def send_q(slot, part, what):
         rows = half(part)
@@ -256,8 +256,8 @@
         src, dst = KV.at[2 - what, what, rows], KV.at[3, what, rows]
         return remote(src, dst, s_k.at[3, part, what], r_k.at[3, part, what], k_dev[2 - what])
 
-    def add_block(qs, q_lo, ks, k_lo, mask, heads=(0, 1)):
-        q_rows, k_rows = pl.ds(q_lo, HALF), pl.ds(k_lo, HALF)
+    def add_block(qs, q_lo, ks, k_lo, mask, queries=HALF, keys=HALF):
+        q_rows, k_rows = pl.ds(q_lo, queries), pl.ds(k_lo, keys)
         dq, dk, dv = block(
             QD[qs, 0, q_rows, :],
             QD[qs, 1, q_rows, :],
@@ -265,42 +265,51 @@
             KV[ks, 0, k_rows, :],
             KV[ks, 1, k_rows, :],
             mask,
-            heads,
+            (0, 1),
         )
         for e, part in dq:
             DQ[qs, e * HEAD : (e + 1) * HEAD, q_rows] += part
         DKV[ks, 0, k_rows, :] += dk
         DKV[ks, 1, k_rows, :] += dv
 
-    def add_either(qs, ks, heads=(0, 1)):
+    def visible_lower(qs, ks):
         q_outer = ((x_hi + qs // 2) % 2) * 2 + (core + qs % 2) % 2
         k_inner = (inner + (ks + 1) // 2 + 2 * ((ks % 2) * (1 - ks // 2))) % 4
-        sel = order[2 * (k_inner * 4 + outer)] < order[2 * (inner * 4 + q_outer)]
+        return order[2 * (k_inner * 4 + outer)] < order[2 * (inner * 4 + q_outer)]
+
+    def add_pair(qs, ks, heads=(0, 1)):
+        sel = visible_lower(qs, ks)
 
         def pick(lo, hi):
             return jnp.where(sel, lo, hi)
 
-        dq, dk, dv = block(
-            pick(QD[qs, 0, 0:HALF, :], QD[qs, 0, HALF:ROWS, :]),
-            pick(QD[qs, 1, 0:HALF, :], QD[qs, 1, HALF:ROWS, :]),
-            pick(ST[qs, :, 0:HALF], ST[qs, :, HALF:ROWS]),
-            pick(KV[ks, 0, 0:HALF, :], KV[ks, 0, HALF:ROWS, :]),
-            pick(KV[ks, 1, 0:HALF, :], KV[ks, 1, HALF:ROWS, :]),
+        q, do, stats = QD[qs, 0], QD[qs, 1], ST[qs]
+        k, v = KV[ks, 0], KV[ks, 1]
+        dq, dk, dv = block(q[HALF:], do[HALF:], stats[:, HALF:], k[:HALF], v[:HALF], False, heads)
+        dq2, dk2, dv2 = block(
+            pick(q[:HALF], q[HALF:]),
+            pick(do[:HALF], do[HALF:]),
+            pick(stats[:, :HALF], stats[:, HALF:]),
+            pick(k[:HALF], k[HALF:]),
+            pick(v[:HALF], v[HALF:]),
             False,
             heads,
         )
-        for e, part in dq:
+        for (e, upper), (_, part) in zip(dq, dq2):
             zero = jnp.zeros_like(part)
             rows = slice(e * HEAD, (e + 1) * HEAD)
             DQ[qs, rows, 0:HALF] += jnp.where(sel, part, zero)
-            DQ[qs, rows, HALF:ROWS] += jnp.where(sel, zero, part)
-        for j, part in enumerate((dk, dv)):
+            DQ[qs, rows, HALF:ROWS] += upper + jnp.where(sel, zero, part)
+        for j, (lower, part) in enumerate(((dk, dk2), (dv, dv2))):
             zero = jnp.zeros_like(part)
-            DKV[ks, j, 0:HALF, :] += jnp.where(sel, part, zero)
+            DKV[ks, j, 0:HALF, :] += lower + jnp.where(sel, part, zero)
             DKV[ks, j, HALF:ROWS, :] += jnp.where(sel, zero, part)
 
-    def add_full(qs, ks, heads=(0, 1)):
-        add_block(qs, HALF, ks, 0, False, heads)
+    def own_diagonal(which):
+        at = pl.multiple_of(which * HALF, HALF)
+        add_block(0, at, 0, at, True, HALF, TILE)
+        at = pl.multiple_of(which * HALF + TILE, TILE)
+        add_block(0, at, 0, at, True, TILE, TILE)
 
     def wait_half(part, kinds):
         base = 4 * ((1 - x_lo) if part == HI else x_lo)
@@ -321,11 +330,13 @@
             send_k(3, part, 2 - slot).start()
 
     for r in turn:
+        exchange(1, r).wait_send()
+    for r in (1, 3, 2, 4, 5, 7, 6):
         for i in (0, 1):
             if r < 4:
                 fetch(r, i).wait()
-        exchange(1, r).wait_send()
         exchange(0, r).start()
+    lax.fori_loop(0, 8, clear, 0)
     for i in range(4):
         fetch(0, i).wait()
     for part in (LO, HI):
@@ -334,10 +345,14 @@
             send_k(slot, part, 0).start()
     near_keys(LO)
     own_stat.wait()
-    for part in (HI, LO):
-        wait_half(part, (2, 0))
+    for part, group in ((x_lo, (1, 2, 3)), (1 - x_lo, (4, 5, 6, 7))):
+        for r in group:
+            for kind in (2, 0):
+                exchange(kind, r).wait_recv()
         for what in (1, 0):
             send_q(1, part, what).start()
+        if group[0] == 1:
+            own_diagonal(x_lo)
     to_stage().wait_recv()
     for b in (1, 3, 2):
         from_stage(b).start()
@@ -380,18 +395,12 @@
         src, dst = dkv_send.at[slot - 1, j], dkv_recv.at[slot - 1, j]
         return remote(src, dst, s_dk.at[slot, j], r_dk.at[slot, j], back_dev[slot])
 
-    def own_diagonal(i, _):
-        at = pl.multiple_of(i * HALF, HALF)
-        add_block(0, at, 0, at, True)
-        return 0
-
-    lax.fori_loop(0, 2, own_diagonal, 0)
-    add_full(0, 0)
+    own_diagonal(1 - x_lo)
+    add_block(0, HALF, 0, 0, False)
     near_keys(HI)
     for part in (HI, LO):
         arrived_queries(1, part)
-    add_full(1, 0)
-    add_either(1, 0)
+    add_pair(1, 0)
 
     def near_queries(n, _):
         qs, ks = n % 2, 1 + n // 2
@@ -408,8 +417,7 @@
                 for what in range(2):
                     send_k(3, part, what).wait_recv()
 
-        add_full(qs, ks)
-        add_either(qs, ks)
+        add_pair(qs, ks)
         return 0
 
     lax.fori_loop(0, 6, near_queries, 0)
@@ -446,8 +454,7 @@
             for part in (HI, LO):
                 arrived_queries(3, part)
 
-        add_full(qs, ks)
-        add_either(qs, ks)
+        add_pair(qs, ks)
         @pl.when(m == 1)
         def _():
             for e in range(2):
@@ -472,13 +479,11 @@
     lax.fori_loop(0, 6, far_queries, 0)
 
     for e in range(2):
-        add_full(3, 0, (e,))
-        add_either(3, 0, (e,))
+        add_pair(3, 0, (e,))
         return_core(3, e).start()
         if e == 1:
             send_rows(1, 0)
-        add_full(2, 0, (e,))
-        add_either(2, 0, (e,))
+        add_pair(2, 0, (e,))
     send_rows(1, 1)
 
     def give(kind, r):
@@ -534,9 +539,22 @@
             give(kind, r).wait()
 
 
-def copy_kernel(dq, dk, dv, dq_out, dk_out, dv_out):
-    for src, dst in ((dq, dq_out), (dk, dk_out), (dv, dv_out)):
-        dst[...] = src[...]
+def copy_kernel(dq, dk, dv, dq_out, dk_out, dv_out, dq_vm, dk_vm, dv_vm, sem):
+    steps = []
+    for i, (src, via, dst) in enumerate(((dq, dq_vm, dq_out), (dk, dk_vm, dk_out), (dv, dv_vm, dv_out))):
+        for j in range(2):
+            rows = pl.ds(j * PART // 2, PART // 2)
+            n = 2 * i + j
+            arrive = pltpu.make_async_copy(src.at[:, rows], via.at[:, rows], sem.at[0, n])
+            leave = pltpu.make_async_copy(via.at[:, rows], dst.at[:, rows], sem.at[1, n])
+            steps.append((arrive, leave))
+    for arrive, _ in steps:
+        arrive.start()
+    for arrive, leave in steps:
+        arrive.wait()
+        leave.start()
+    for _, leave in steps:
+        leave.wait()
 
 
 def per_device(queries, key_input, value_input, outputs, output_gradient, log_sum_exp, block_order):
@@ -596,12 +614,12 @@
         ),
         name="attention_backward",
     )(block_order, queries, key_input, value_input, outputs, output_gradient, jnp.transpose(log_sum_exp, (0, 2, 1)))
-    whole = pl.BlockSpec(memory_space=pltpu.VMEM)
     return pl.pallas_call(
         copy_kernel,
         out_shape=tuple(jax.ShapeDtypeStruct(g.shape, g.dtype) for g in grads),
-        in_specs=[whole] * 3,
-        out_specs=(whole,) * 3,
+        in_specs=[any_space] * 3,
+        out_specs=(any_space,) * 3,
+        scratch_shapes=[pltpu.VMEM(g.shape, g.dtype) for g in grads] + [dma((2, 6))],
         name="copy_out",
     )(*grads)
 

time: 96.4 us -> 95 us (0.985)
  no operation moved by 1% of the time
where the time goes in v4:
time: 95 us; the launch traced here: 94.8 us
  Pallas kernels  94 us (99%)
    pallas_call x1, Pallas kernels, per_device(): pl.pallas_call(kernel, out_shape=(jax.ShapeDtypeStruct((1, PART, 2048), B...  92 us
    pallas_call x1, Pallas kernels, per_device(): pl.pallas_call(copy_kernel, out_shape=tuple((jax.ShapeDtypeStruct(g.shape...  2.01 us

profile of v4, /device:TPU:0, one launch (start us, length us, event | category | flops | bytes accessed | tf_op | source)
XLA Modules:
  0.0 94.8 jit_solution(16490694894833440711)
XLA Ops:
  0.6 92.0 %attention_backward.1 = (bf16[1,128,2048]{2,1,0:T(8,128)(2,1)}, bf16[1,128,1024]{2,1,0:T(8,128)(2,1)}, bf16[1,128,1024]{2,1,0:T(8,128)(2,1)}) custom-call(s32[32]{0:T(128)} %order.1, bf16[1,128,2048]{2,1,0:T(8,128)(2,1)} %q_in.1, bf16[1,128,1024]{2,1,0:T(8,128)(2,1)} %k_in.1, bf16[1,128,1024]{2,1,0:T(8,128)(2,1)} %v_in.1, bf16[1,128,2048]{2,1,0:T(8,128)(2,1)} %o_in.1, ...), custom_call_target="tpu_custom_call" | custom-call | tf_op jit(solution)/shard_map/attention_backward/pallas_call | solution.py:563
  92.6 2.0 %copy_out.1 = (bf16[1,128,2048]{2,1,0:T(8,128)(2,1)}, bf16[1,128,1024]{2,1,0:T(8,128)(2,1)}, bf16[1,128,1024]{2,1,0:T(8,128)(2,1)}) custom-call(bf16[1,128,2048]{2,1,0:T(8,128)(2,1)} %get-tuple-element.6.dq, bf16[1,128,1024]{2,1,0:T(8,128)(2,1)} %get-tuple-element.7.dk, bf16[1,128,1024]{2,1,0:T(8,128)(2,1)} %get-tuple-element.8.dv), custom_call_target="tpu_custom_call" | custom-call | tf_op jit(solution)/shard_map/copy_out/pallas_call | solution.py:617

commit v5 on v4

--- a/solution.py
+++ b/solution.py
@@ -183,7 +183,7 @@
         device = (x_lo * 4 + (z + b) % 4, inner, outer)
         return remote(far_stage.at[b - 1], QD.at[2, :, rows], s_stage.at[b], r_stage.at[b], device)
 
-    turn = (4, 1, 5, 3, 7, 2, 6)
+    turn = (1, 3, 2, 4, 5, 7, 6)
     for pick in ((2, 3), (0, 1)):
         for r in turn:
             for i in pick:
@@ -339,11 +339,12 @@
     lax.fori_loop(0, 8, clear, 0)
     for i in range(4):
         fetch(0, i).wait()
-    for part in (LO, HI):
-        wait_half(part, (1,))
+    for part, group in ((x_lo, (1, 2, 3)), (1 - x_lo, (4, 5, 6, 7))):
+        for r in group:
+            exchange(1, r).wait_recv()
         for slot in (1, 2):
             send_k(slot, part, 0).start()
-    near_keys(LO)
+    near_keys(x_lo)
     own_stat.wait()
     for part, group in ((x_lo, (1, 2, 3)), (1 - x_lo, (4, 5, 6, 7))):
         for r in group:
@@ -397,7 +398,7 @@
 
     own_diagonal(1 - x_lo)
     add_block(0, HALF, 0, 0, False)
-    near_keys(HI)
+    near_keys(1 - x_lo)
     for part in (HI, LO):
         arrived_queries(1, part)
     add_pair(1, 0)

time: 95 us -> 95 us (level)
  no operation moved by 1% of the time
where the time goes in v5:
time: 95 us; the launch traced here: 94.8 us
  Pallas kernels  94 us (99%)
    pallas_call x1, Pallas kernels, per_device(): pl.pallas_call(kernel, out_shape=(jax.ShapeDtypeStruct((1, PART, 2048), B...  92 us
    pallas_call x1, Pallas kernels, per_device(): pl.pallas_call(copy_kernel, out_shape=tuple((jax.ShapeDtypeStruct(g.shape...  2.01 us

profile of v5, /device:TPU:0, one launch (start us, length us, event | category | flops | bytes accessed | tf_op | source)
XLA Modules:
  0.0 94.8 jit_solution(11091525807039923497)
XLA Ops:
  0.6 92.0 %attention_backward.1 = (bf16[1,128,2048]{2,1,0:T(8,128)(2,1)}, bf16[1,128,1024]{2,1,0:T(8,128)(2,1)}, bf16[1,128,1024]{2,1,0:T(8,128)(2,1)}) custom-call(s32[32]{0:T(128)} %order.1, bf16[1,128,2048]{2,1,0:T(8,128)(2,1)} %q_in.1, bf16[1,128,1024]{2,1,0:T(8,128)(2,1)} %k_in.1, bf16[1,128,1024]{2,1,0:T(8,128)(2,1)} %v_in.1, bf16[1,128,2048]{2,1,0:T(8,128)(2,1)} %o_in.1, ...), custom_call_target="tpu_custom_call" | custom-call | tf_op jit(solution)/shard_map/attention_backward/pallas_call | solution.py:564
  92.6 2.0 %copy_out.1 = (bf16[1,128,2048]{2,1,0:T(8,128)(2,1)}, bf16[1,128,1024]{2,1,0:T(8,128)(2,1)}, bf16[1,128,1024]{2,1,0:T(8,128)(2,1)}) custom-call(bf16[1,128,2048]{2,1,0:T(8,128)(2,1)} %get-tuple-element.6.dq, bf16[1,128,1024]{2,1,0:T(8,128)(2,1)} %get-tuple-element.7.dk, bf16[1,128,1024]{2,1,0:T(8,128)(2,1)} %get-tuple-element.8.dv), custom_call_target="tpu_custom_call" | custom-call | tf_op jit(solution)/shard_map/copy_out/pallas_call | solution.py:618
